TPU v7x, 256 devices: a whole 4x4x8 slice. The times are simulated.
256 devices in a mesh: tm: 4 (over y), row: 8 (over z_lo, core), col: 8 (over z_hi, x).
Axes of the slice: x: 4, y: 4, z: 8 (z_hi: 2, z_lo: 4; z = z_hi * 4 + z_lo), core: 2. Of those that a mesh axis runs over, the one named last changes fastest.
Arguments:
- states: float32 [4, 1280, 3072], P('tm', 'row', 'col'), may hold values from -45 to 45
- anchor: float32 [1280, 3072], P('row', 'col'), may hold values from -2.25 to 2.25
- timesteps: int32 [4], P('tm'), may hold values from 0 to 999
- step_sizes: float32 [4], P('tm'), may hold values from 0.25 to 1
- weight_in: bfloat16 [3072, 12288], P('col', 'row'), may hold values from -0.109375 to 0.109375
- weight_out: bfloat16 [12288, 3072], P('row', 'col'), may hold values from -0.0546875 to 0.0546875
- mod_weight: bfloat16 [3072, 3, 3072], P('row', None, 'col'), may hold values from -0.109375 to 0.109375
Outputs:
- advanced: float32 [4, 1280, 3072], P('tm', 'row', 'col')
All inputs are finite; a program needn't handle non-finite values.
Results may differ from a plain program's by a relative error of at most 0.028.
Values may be sent and summed in bfloat16 or wider, within the bound.
A program may use at most 64 MiB of HBM per device.

v0:
```python
import math

import jax
import jax.numpy as jnp
from jax import lax
from jax.sharding import PartitionSpec as P

D = 3072
ITERS = 2


EPSILON = 1e-06


def entering(shard, axis, combine, identity):
    count, here = (lax.axis_size(axis), lax.axis_index(axis))
    everything = lax.all_gather(shard.astype(jnp.bfloat16), axis)
    start = jnp.broadcast_to(jnp.asarray(identity, shard.dtype), shard.shape)

    def step(k, before):
        reached = k < here
        new = combine(before, everything[k].astype(shard.dtype))
        return jnp.where(reached, new, before)

    return lax.fori_loop(0, count, step, start)


def timestep_embedding(timesteps):
    half_width = D // 2
    positions = jnp.arange(half_width, dtype=jnp.float32)
    frequency = jnp.exp(-math.log(10000.0) * positions / half_width)
    phases = timesteps.astype(jnp.float32)[:, None] * frequency[None, :]
    return jnp.concatenate([jnp.cos(phases), jnp.sin(phases)], axis=1)


def local(states, anchor, timesteps, step_sizes, weight_in, weight_out, mod_weight):
    embedding = timestep_embedding(timesteps)[0]
    rows_here = mod_weight.shape[0]
    embed_part = lax.dynamic_slice_in_dim(
        embedding, lax.axis_index("row") * rows_here, rows_here, 0
    )
    mod_part = jnp.einsum(
        "e,ekd->kd", embed_part, mod_weight.astype(jnp.float32), precision=lax.Precision.HIGHEST
    )
    modulation = lax.psum(mod_part, "row")
    shift_mod = modulation[0]
    scale_mod = modulation[1]
    gate_mod = modulation[2]
    step_size = step_sizes[0]
    current = states[0]
    for sweep in range(ITERS):
        row_sum = jnp.sum(current, axis=1)
        squares = jnp.sum(current * current, axis=1)
        row_sum, squares = lax.psum((row_sum, squares), "col")
        row_mean = row_sum / D
        row_var = squares / D - row_mean * row_mean
        normed = (
            (current - row_mean[:, None])
            * lax.rsqrt(row_var + EPSILON)[:, None]
            * (1.0 + scale_mod)
            + shift_mod
        ).astype(jnp.bfloat16)
        panels_all = lax.all_gather(normed, "row", axis=0, tiled=True)
        pre_share = lax.psum_scatter(
            jnp.dot(panels_all, weight_in, preferred_element_type=jnp.float32).astype(jnp.bfloat16),
            "col",
            scatter_dimension=0,
            tiled=True,
        ).astype(jnp.float32)
        hidden_share = jax.nn.gelu(pre_share, approximate=True).astype(jnp.bfloat16)
        hidden = lax.all_gather(hidden_share, "col", axis=0, tiled=True)
        block_out = lax.psum_scatter(
            jnp.dot(hidden, weight_out, preferred_element_type=jnp.float32).astype(jnp.bfloat16),
            "row",
            scatter_dimension=0,
            tiled=True,
        ).astype(jnp.float32)
        drift_term = step_size * gate_mod * block_out
        prefix = entering(
            drift_term,
            "tm",
            lambda earlier, later: earlier + later,
            jnp.zeros(drift_term.shape, jnp.float32),
        )
        if sweep + 1 < ITERS:
            current = anchor + prefix
        else:
            advanced = anchor + prefix + drift_term
    return advanced[None]


def solution(mesh):
    placed = (
        P("tm", "row", "col"),
        P("row", "col"),
        P("tm"),
        P("tm"),
        P("col", "row"),
        P("row", "col"),
        P("row", None, "col"),
    )
    return jax.shard_map(
        local, mesh=mesh, in_specs=placed, out_specs=P("tm", "row", "col"), check_vma=False
    )
```

profile of v0, /device:TPU:17, one launch (start us, length us, event | category | flops | bytes accessed | tf_op | source)
XLA Modules:
  0.0 675.7 jit_solution(1032973711250415376)
XLA Ops:
  6.5 0.0 copy-start
  6.5 0.0 reduce-scatter.5.cloned.1.call-start
  7.3 0.2 fusion.18
  7.5 1.6 fusion.23
  9.1 15.0 %psum.35 = f32[3,384]{1,0:T(4,128)S(1)} all-reduce(f32[3,384]{1,0:T(4,128)S(1)} %bitcast.47), channel_id=1, replica_groups=mesh['tm'=4,'row'=8,'col'=8] {'row'}, use_global_device_ids=true, to_apply=%region_0.0 | all-reduce | flops 1152 | bytes 9216 | tf_op jit(solution)/shard_map/psum | solution.py:45
  24.8 1.1 fusion.16
  25.9 1.1 reduce_sum.36
  27.0 28.2 %all-reduce.1 = (f32[160]{0:T(256)S(1)}, f32[160]{0:T(256)S(1)}) all-reduce(f32[160]{0:T(256)S(1)} %fusion.16, f32[160]{0:T(256)S(1)} %reduce_sum.36), channel_id=1, replica_groups=mesh['tm'=4,'row'=8,'col'=8] {'col'}, use_global_device_ids=true, to_apply=%region_4.0 | all-reduce | flops 320 | bytes 2560 | tf_op jit(solution)/shard_map/psum | solution.py:54
  55.2 1.1 fusion.15
  56.3 21.9 %all_gather.24 = bf16[1280,384]{1,0:T(8,128)(2,1)S(1)} all-gather(bf16[160,384]{1,0:T(8,128)(2,1)S(1)} %fusion.15), channel_id=1, replica_groups=mesh['tm'=4,'row'=8,'col'=8] {'row'}, dimensions={0}, use_global_device_ids=true | all-gather | bytes 1105920 | tf_op jit(solution)/shard_map/all_gather | solution.py:63
  78.1 0.0 copy-done
  78.1 4.1 convolution_convert_fusion.1
  82.2 0.0 copy-start.3
  82.2 0.0 reduce-scatter.5.cloned.1.call-update
  82.2 0.0 all-gather.5.cloned.1.call-start
  82.3 115.9 %reduce-scatter.5.cloned.1.call-done = bf16[160,1536]{1,0:T(8,128)(2,1)} async-done(((bf16[1280,1536]{1,0:T(8,128)(2,1)}), bf16[160,1536]{1,0:T(8,128)(2,1)}) %reduce-scatter.5.cloned.1.call-update) | async-done | bytes 491536 | tf_op jit(solution)/shard_map/reduce_scatter | solution.py:64
  198.2 2.2 fusion.5
  200.4 0.0 all-gather.5.cloned.1.call-update
  200.4 0.0 reduce-scatter.7.cloned.1.call-start
  200.5 93.8 %all-gather.5.cloned.1.call-done = bf16[1280,1536]{1,0:T(8,128)(2,1)} async-done(((bf16[160,1536]{1,0:T(8,128)(2,1)}), bf16[1280,1536]{1,0:T(8,128)(2,1)}) %all-gather.5.cloned.1.call-update) | async-done | bytes 3932176 | tf_op jit(solution)/shard_map/all_gather | solution.py:71
  294.3 0.0 copy-done.3
  294.3 5.3 convolution_convert_fusion.3
  299.6 0.0 reduce-scatter.7.cloned.1.call-update
  299.6 0.0 reduce-scatter.9.cloned.1.call-start
  299.6 35.6 %reduce-scatter.7.cloned.1.call-done = bf16[160,384]{1,0:T(8,128)(2,1)} async-done(((bf16[1280,384]{1,0:T(8,128)(2,1)}), bf16[160,384]{1,0:T(8,128)(2,1)}) %reduce-scatter.7.cloned.1.call-update) | async-done | bytes 122896 | tf_op jit(solution)/shard_map/reduce_scatter | solution.py:72
  335.2 0.9 multiply_convert_fusion
  336.1 0.0 copy-start.1
  336.2 9.2 %all-gather = bf16[640,384]{1,0:T(8,128)(2,1)S(1)} all-gather(bf16[160,384]{1,0:T(8,128)(2,1)S(1)} %multiply_convert_fusion), channel_id=2, replica_groups=mesh['tm'=4,'row'=8,'col'=8] {'tm'}, dimensions={0}, use_global_device_ids=true | all-gather | bytes 614400 | tf_op jit(solution)/shard_map/all_gather | solution.py:17
  345.4 0.4 while.28
  345.4 0.1 add_select_fusion.4
  345.5 0.1 add_select_fusion.4
  345.6 0.1 add_select_fusion.4
  345.7 0.1 add_select_fusion.4
  345.8 0.0 copy-done.1
  345.8 0.2 fusion.28
  346.0 28.8 %all-reduce = (f32[160]{0:T(256)S(1)}, f32[160]{0:T(256)S(1)}) all-reduce(f32[160]{0:T(256)S(1)} %get-tuple-element.196, f32[160]{0:T(256)S(1)} %get-tuple-element.195), channel_id=1, replica_groups=mesh['tm'=4,'row'=8,'col'=8] {'col'}, use_global_device_ids=true, to_apply=%region_12.13 | all-reduce | flops 320 | bytes 2560 | tf_op jit(solution)/shard_map/psum | solution.py:54
  374.8 0.1 add_convert_fusion
  374.9 23.1 %all_gather.28 = bf16[1280,384]{1,0:T(8,128)(2,1)S(1)} all-gather(bf16[160,384]{1,0:T(8,128)(2,1)S(1)} %add_convert_fusion), channel_id=1, replica_groups=mesh['tm'=4,'row'=8,'col'=8] {'row'}, dimensions={0}, use_global_device_ids=true | all-gather | bytes 1105920 | tf_op jit(solution)/shard_map/all_gather | solution.py:63
  398.0 4.1 convolution_convert_fusion
  402.1 0.0 reduce-scatter.9.cloned.1.call-update
  402.1 0.0 all-gather.7.cloned.1.call-start
  402.2 118.6 %reduce-scatter.9.cloned.1.call-done = bf16[160,1536]{1,0:T(8,128)(2,1)} async-done(((bf16[1280,1536]{1,0:T(8,128)(2,1)}), bf16[160,1536]{1,0:T(8,128)(2,1)}) %reduce-scatter.9.cloned.1.call-update) | async-done | bytes 491536 | tf_op jit(solution)/shard_map/reduce_scatter | solution.py:64
  520.8 2.2 fusion.11
  523.0 0.0 all-gather.7.cloned.1.call-update
  523.0 0.0 reduce-scatter.11.cloned.1.call-start
  523.0 93.7 %all-gather.7.cloned.1.call-done = bf16[1280,1536]{1,0:T(8,128)(2,1)} async-done(((bf16[160,1536]{1,0:T(8,128)(2,1)}), bf16[1280,1536]{1,0:T(8,128)(2,1)}) %all-gather.7.cloned.1.call-update) | async-done | bytes 3932176 | tf_op jit(solution)/shard_map/all_gather | solution.py:71
  616.7 5.3 convolution_convert_fusion.2
  622.0 0.0 reduce-scatter.11.cloned.1.call-update
  622.0 35.6 %reduce-scatter.11.cloned.1.call-done = bf16[160,384]{1,0:T(8,128)(2,1)} async-done(((bf16[1280,384]{1,0:T(8,128)(2,1)}), bf16[160,384]{1,0:T(8,128)(2,1)}) %reduce-scatter.11.cloned.1.call-update) | async-done | bytes 122896 | tf_op jit(solution)/shard_map/reduce_scatter | solution.py:72
  657.6 0.9 fusion.17
  658.5 0.0 copy-start.2
  658.5 9.1 %all-gather.1 = bf16[640,384]{1,0:T(8,128)(2,1)S(1)} all-gather(bf16[160,384]{1,0:T(8,128)(2,1)S(1)} %fusion.17), channel_id=3, replica_groups=mesh['tm'=4,'row'=8,'col'=8] {'tm'}, dimensions={0}, use_global_device_ids=true | all-gather | bytes 614400 | tf_op jit(solution)/shard_map/all_gather | solution.py:17
  667.7 0.4 while.29
  667.7 0.1 add_select_fusion.5
  667.8 0.1 add_select_fusion.5
  667.9 0.1 add_select_fusion.5
  668.0 0.1 add_select_fusion.5
  668.1 0.0 copy-done.2
  668.1 0.7 add_bitcast_fusion
  (6 shorter events, 0.1 us)
Async XLA Ops:
  6.5 71.6 %copy-start = (bf16[384,1536]{1,0:T(8,128)(2,1)S(1)}, bf16[384,1536]{1,0:T(8,128)(2,1)}, u32[]{:S(2)}) copy-start(bf16[384,1536]{1,0:T(8,128)(2,1)} %param.15) | copy-start | bytes 3538948
  6.5 191.7 %reduce-scatter.5.cloned.1.call-start = ((), (), s32[]{:S(2)}) async-start(), calls=%async_computation.4 | async-start | bytes 4423680 | tf_op jit(solution)/shard_map/reduce_scatter | solution.py:64
  82.2 212.1 %copy-start.3 = (bf16[1536,384]{1,0:T(8,128)(2,1)S(1)}, bf16[1536,384]{1,0:T(8,128)(2,1)}, u32[]{:S(2)}) copy-start(bf16[1536,384]{1,0:T(8,128)(2,1)} %param.16) | copy-start | bytes 3538948
  82.2 212.0 %all-gather.5.cloned.1.call-start = ((), (), s32[]{:S(2)}) async-start(), calls=%async_computation.5 | async-start | bytes 4423680 | tf_op jit(solution)/shard_map/all_gather | solution.py:71
  200.4 134.8 %reduce-scatter.7.cloned.1.call-start = ((), (), s32[]{:S(2)}) async-start(), calls=%async_computation.6 | async-start | bytes 1105920 | tf_op jit(solution)/shard_map/reduce_scatter | solution.py:72
  299.6 221.2 %reduce-scatter.9.cloned.1.call-start = ((), (), s32[]{:S(2)}) async-start(), calls=%async_computation.7 | async-start | bytes 4423680 | tf_op jit(solution)/shard_map/reduce_scatter | solution.py:64
  336.1 9.6 %copy-start.1 = (f32[160,384]{1,0:T(8,128)S(1)}, f32[160,384]{1,0:T(8,128)}, u32[]{:S(2)}) copy-start(f32[160,384]{1,0:T(8,128)} %param.12) | copy-start | bytes 737284
  402.1 214.6 %all-gather.7.cloned.1.call-start = ((), (), s32[]{:S(2)}) async-start(), calls=%async_computation.8 | async-start | bytes 4423680 | tf_op jit(solution)/shard_map/all_gather | solution.py:71
  523.0 134.6 %reduce-scatter.11.cloned.1.call-start = ((), (), s32[]{:S(2)}) async-start(), calls=%async_computation.9 | async-start | bytes 1105920 | tf_op jit(solution)/shard_map/reduce_scatter | solution.py:72
  658.5 9.5 %copy-start.2 = (bf16[160,384]{1,0:T(8,128)(2,1)S(1)}, bf16[160,384]{1,0:T(8,128)(2,1)}, u32[]{:S(2)}) copy-start(bf16[160,384]{1,0:T(8,128)(2,1)} %reduce-scatter.11.cloned.1.call-done) | copy-start | bytes 368644
Sparse Core Ops, SparseCore 0:
  82.4 115.8 reduce-scatter.4
  201.2 93.0 all-gather.4
  299.7 35.4 reduce-scatter.6
  402.3 118.5 reduce-scatter.8
  523.6 93.0 all-gather.6
  622.1 35.4 reduce-scatter.10
where the time goes:
time: 685 us; the launch traced here: 676 us
  waiting for transfers between devices  493 us (72%)
  blocking collectives  135 us (20%)
  matrix products  20.4 us (3%)
  between operations  15 us (2%)
  other arithmetic  11.3 us (2%)
    reduce_scatter x2, waiting for transfers between devices, local(): lax.psum_scatter(jnp.dot(panels_all, weight_in, preferred_element_type=jn...  235 us
    all_gather x2, waiting for transfers between devices, local(): hidden = lax.all_gather(hidden_share, 'col', axis=0, tiled=True)  187 us
    reduce_scatter x2, waiting for transfers between devices, local(): lax.psum_scatter(jnp.dot(hidden, weight_out, preferred_element_type=jnp.f...  71.2 us
    psum x2, blocking collectives, local(): row_sum, squares = lax.psum((row_sum, squares), 'col')  57 us
    all_gather x2, blocking collectives, local(): panels_all = lax.all_gather(normed, 'row', axis=0, tiled=True)  45 us
    all_gather x2, blocking collectives, entering(): everything = lax.all_gather(shard.astype(jnp.bfloat16), axis)  18.3 us
    psum x1, blocking collectives, local(): modulation = lax.psum(mod_part, 'row')  15 us
  transfers between devices with their start and end apart: 6, of which 6 were waited for; matrix products, arithmetic and copies ran while one was open for 0% of the time, Pallas kernels for 0%

commit v1 on v0

v1 whole, which is shorter than its diff:
```python
import functools
import math

import jax
import jax.numpy as jnp
from jax import lax
from jax.experimental import pallas as pl
from jax.experimental.pallas import tpu as pltpu
from jax.sharding import PartitionSpec as P

D = 3072
ITERS = 2
EPSILON = 1e-06
MESH = pl.DeviceIdType.MESH
F32 = jnp.float32
BF16 = jnp.bfloat16

T = 80
W = 384
U = 768

COPIES = 192


def timestep_embedding(timesteps):
    half_width = D // 2
    positions = jnp.arange(half_width, dtype=jnp.float32)
    frequency = jnp.exp(-math.log(10000.0) * positions / half_width)
    phases = timesteps.astype(jnp.float32)[:, None] * frequency[None, :]
    return jnp.concatenate([jnp.cos(phases), jnp.sin(phases)], axis=1)


def kernel(
    step_ref, s_ref, a_ref, m_ref, wi_ref, wo_ref, out_ref,
    sbuf, abuf, mbuf, m1, m2, mrecv, modall, stat, statr,
    xall, win, wout, hid, obs, obr, part, rss, rsr, dsend, drecv, pref, fsend, frecv,
    send, recv,
):
    y = lax.axis_index("tm")
    row = lax.axis_index("row")
    col = lax.axis_index("col")
    l, c = row // 2, lax.rem(row, 2)
    h, x = col // 4, lax.rem(col, 4)
    z = 4 * h + l

    def dev(x_=None, y_=None, z_=None, c_=None):
        x_ = x if x_ is None else x_
        y_ = y if y_ is None else y_
        z_ = z if z_ is None else z_
        c_ = c if c_ is None else c_
        return (y_, 2 * lax.rem(z_, 4) + c_, 4 * (z_ // 4) + x_)

    def xo(k):
        return lax.rem(x + k + 4, 4)

    def yo(k):
        return lax.rem(y + k + 4, 4)

    def zo(k):
        return lax.rem(z + k + 8, 8)

    sib = dev(c_=1 - c)
    z4 = dev(z_=zo(4))
    z4sib = dev(z_=zo(4), c_=1 - c)

    def lo(k):
        return dev(z_=4 * h + lax.rem(l + k, 4))

    ids = iter(range(COPIES))
    pending = []

    def remote(src, dst, ss, rs, to):
        return pltpu.make_async_remote_copy(
            src_ref=src, dst_ref=dst, send_sem=send.at[ss], recv_sem=recv.at[rs],
            device_id=to, device_id_type=MESH,
        )

    def put(k, src, dst, to):
        copy = remote(src, dst, k, k, to)
        copy.start()
        pending.append(copy)

    def got(k, dst):
        remote(dst, dst, k, k, sib).wait_recv()

    partners = [sib, z4, z4sib, dev(z_=zo(1)), dev(z_=zo(-1))]
    partners += [dev(x_=xo(k)) for k in (1, 2, 3)]
    partners += [dev(y_=yo(k)) for k in (1, 2, 3)]
    partners += [lo(k) for k in (1, 2, 3)]
    barrier = pltpu.get_barrier_semaphore()
    for p in partners:
        pl.semaphore_signal(barrier, inc=1, device_id=p, device_id_type=MESH)
    half = lax.rem(x, 2)
    same = x // 2 == c
    swap = [dev(x_=2 * c + i, c_=x // 2) for i in range(2)]
    own = [jnp.logical_and(same, half == i) for i in range(2)]
    for i in range(2):

        @pl.when(jnp.logical_not(own[i]))
        def _(i=i):
            pl.semaphore_signal(barrier, inc=1, device_id=swap[i], device_id_type=MESH)

    pl.semaphore_wait(barrier, len(partners) + 2 - same.astype(jnp.int32))

    swaps = []

    def swap_out(src_of, dst):
        ks = (next(ids), next(ids))
        for i in range(2):

            @pl.when(own[i])
            def _(i=i):
                pltpu.make_async_copy(src_of(i), dst.at[half], recv.at[ks[0] + half]).start()

            @pl.when(jnp.logical_not(own[i]))
            def _(i=i):
                remote(src_of(i), dst.at[half], ks[i], ks[0] + half, swap[i]).start()

        swaps.append((ks, src_of, dst))
        return ks

    def swap_in(ks, dst):
        for i in range(2):
            got(ks[i], dst.at[i])

    ks_state = swap_out(lambda i: s_ref.at[pl.ds(T * i, T)], sbuf)

    mbuf[...] = jnp.zeros_like(mbuf)
    mbuf[0:3, :] = m_ref[...]
    k_ms = next(ids)
    put(k_ms, mbuf, mrecv.at[0], sib)

    mine = 4 * h + x
    far = 4 * (1 - h)

    def win_slot(hx, first=0, rows=W):
        return win.at[pl.ds(pl.multiple_of(hx * W + first, 16), rows), :]

    def wout_slot(hx, first=0, rows=U):
        return wout.at[
            hx // 2, pl.ds(pl.multiple_of(first, 16), rows), pl.ds(pl.multiple_of(lax.rem(hx, 2) * W, 128), W)
        ]

    def wi_part(hd, first, rows):
        return wi_ref.at[pl.ds(pl.multiple_of(first, 16), rows), pl.ds(pl.multiple_of(hd * U, 128), U)]

    def wo_part(hd, first, rows):
        return wo_ref.at[pl.ds(pl.multiple_of(hd * U + first, 16), rows), :]

    sides = ((wi_part, win_slot, W), (wo_part, wout_slot, U))
    ids_w = []
    local = []
    for part_of, slot_of, rows in sides:
        k_x = {k: next(ids) for k in (1, 3)}
        k_fwd = {k: next(ids) for k in (1, 3)}
        k_z = next(ids)
        k_xq = {k: next(ids) for k in (1, 2, 3)}
        k_y = {(s, k): next(ids) for s in range(4) for k in (1, 2, 3)}
        k_own = next(ids)
        ids_w.append((k_x, k_fwd, k_z, k_xq, k_y, k_own))

    def weight_start(w):
        part_of, slot_of, rows = sides[w]
        k_x, k_fwd, k_z, k_xq, k_y, k_own = ids_w[w]
        q = rows // 4
        put(k_z, part_of(1 - h, y * q, q), slot_of(mine, y * q, q), z4)
        for k in (1, 3):
            put(k_x[k], part_of(h, 0, rows), slot_of(mine), dev(x_=xo(k)))
        copy = pltpu.make_async_copy(part_of(h, 0, rows), slot_of(mine), recv.at[k_own])
        copy.start()
        local.append(copy)

    def weight_far(w):
        part_of, slot_of, rows = sides[w]
        k_x, k_fwd, k_z, k_xq, k_y, k_own = ids_w[w]
        q = rows // 4
        here = slot_of(far + x, y * q, q)
        got(k_z, here)
        for k in (1, 3, 2):
            put(k_xq[k], here, here, dev(x_=xo(k)))
        for k in (1, 3, 2):
            put(k_y[0, k], here, here, dev(y_=yo(k)))

    def weight_far_x(w, s):
        part_of, slot_of, rows = sides[w]
        k_x, k_fwd, k_z, k_xq, k_y, k_own = ids_w[w]
        q = rows // 4
        here = slot_of(far + xo(-s), y * q, q)
        got(k_xq[s], here)
        for k in (1, 3, 2):
            put(k_y[s, k], here, here, dev(y_=yo(k)))

    def weight_near(w):
        part_of, slot_of, rows = sides[w]
        k_x, k_fwd, k_z, k_xq, k_y, k_own = ids_w[w]
        for k, first in ((1, 0), (3, rows // 2)):
            got(k_x[k], slot_of(4 * h + xo(-k)))
            there = slot_of(4 * h + xo(-k), first, rows // 2)
            put(k_fwd[k], there, there, dev(x_=xo(k)))

    def weight_end(w):
        part_of, slot_of, rows = sides[w]
        k_x, k_fwd, k_z, k_xq, k_y, k_own = ids_w[w]
        q = rows // 4
        for k, first in ((1, 0), (3, rows // 2)):
            got(k_fwd[k], slot_of(4 * h + xo(2), first, rows // 2))
        for s in range(4):
            for k in (1, 2, 3):
                got(k_y[s, k], slot_of(far + xo(-s), yo(-k) * q, q))
        local[w].wait()

    weight_start(0)
    ks_anchor = swap_out(lambda i: a_ref.at[pl.ds(T * i, T)], abuf)
    weight_start(1)

    def stats_send(it, cur):
        total = sum(jnp.sum(v, axis=1, keepdims=True) for v in cur)
        squares = sum(jnp.sum(v * v, axis=1, keepdims=True) for v in cur)
        lane = lax.broadcasted_iota(jnp.int32, (T, 128), 1)
        stat[it] = jnp.where(lane < 64, total, squares)
        ks = [next(ids) for _ in range(3)]
        for k, to in zip(ks, (z4, z4sib, sib)):
            put(k, stat.at[it], statr.at[it, ks.index(k)], to)
        return ks

    def mod(j, r):
        return modall[2 * c + j, r : r + 1, :]

    def x_slot(it, zz, cc, j):
        hh, ll = zz // 4, lax.rem(zz, 4)
        return xall.at[
            it,
            pl.ds(pl.multiple_of(ll * T, 16), T),
            pl.ds(pl.multiple_of((4 * hh + 2 * cc + j) * W, 128), W),
        ]

    def normalise(it, cur, ks):
        for i, k in enumerate(ks):
            got(k, statr.at[it, i])
        total = stat[it] + statr[it, 0] + statr[it, 1] + statr[it, 2]
        mean = total[:, 0:1] / D
        var = total[:, 64:65] / D - mean * mean
        scale = lax.rsqrt(var + EPSILON)
        for j in range(2):
            value = (cur[j] - mean) * scale * (1.0 + mod(j, 1)) + mod(j, 0)
            xall[
                it,
                pl.ds(pl.multiple_of(l * T, 16), T),
                pl.ds(pl.multiple_of((4 * h + 2 * c + j) * W, 128), W),
            ] = value.astype(BF16)

    def ring_dirs(s):
        return [(g, j) for j in range(2) for g in (0, 1) if s < 4 or g == j]

    sign = (1, -1)

    class Gather:
        def __init__(self, it):
            self.it = it
            self.k = {(s, g, j): next(ids) for s in range(1, 5) for g, j in ring_dirs(s)}
            self.ks = {(s, g, j): next(ids) for s in range(1, 5) for g, j in ring_dirs(s)}
            self.k0 = [next(ids) for _ in range(2)]

        def first(self):
            for j in range(2):
                slot = x_slot(self.it, z, c, j)
                for g in range(2):
                    put(self.k[1, g, j], slot, slot, dev(z_=zo(sign[g])))
                put(self.k0[j], slot, slot, sib)

        def step(self, s):
            for g, j in ring_dirs(s):
                slot = x_slot(self.it, zo(-sign[g] * s), c, j)
                got(self.k[s, g, j], slot)
                if (s + 1, g, j) in self.k:
                    put(self.k[s + 1, g, j], slot, slot, dev(z_=zo(sign[g])))
                put(self.ks[s, g, j], slot, slot, sib)

        def end(self):
            for j in range(2):
                got(self.k0[j], x_slot(self.it, z, 1 - c, j))
            for s in range(1, 5):
                for g, j in ring_dirs(s):
                    got(self.ks[s, g, j], x_slot(self.it, zo(-sign[g] * s), 1 - c, j))

    def first_matmul(it):
        def tile(n, _):
            cols = pl.ds(pl.multiple_of(n * 256, 256), 256)
            pre = jnp.dot(xall[it], win[:, cols], preferred_element_type=F32)
            hid[:, cols] = jax.nn.gelu(pre, approximate=True).astype(BF16)
            return 0

        lax.fori_loop(0, U // 256, tile, 0)

    def second_matmul(it):
        ks = [next(ids) for _ in range(2)]
        for hh in range(2):

            def tile(n, _, hh=hh):
                cols = pl.ds(pl.multiple_of(n * 256, 256), 256)
                other = jnp.dot(hid[...], wout[2 * hh + 1 - c, :, cols], preferred_element_type=F32)
                obs[it, hh, :, cols] = other.astype(BF16)
                return 0

            lax.fori_loop(0, 3, tile, 0)
            put(ks[hh], obs.at[it, hh], obr.at[it, hh], sib)
        for hh in range(2):

            def tile(n, _, hh=hh):
                cols = pl.ds(pl.multiple_of(n * 256, 256), 256)
                kept = jnp.dot(hid[...], wout[2 * hh + c, :, cols], preferred_element_type=F32)
                part[hh, :, :, cols] = kept.reshape(4, T, 256)
                return 0

            lax.fori_loop(0, 3, tile, 0)
        for hh in range(2):
            got(ks[hh], obr.at[it, hh])
            part[hh] += obr[it, hh].astype(F32).reshape(4, T, 2 * W)

    def scatter(it):
        k = {(s, g, j): next(ids) for s in range(1, 5) for g in range(2) for j in range(2) if s > 1 or g == j}

        def term(d, j):
            return part[d // 4, lax.rem(d, 4), :, W * j : W * (j + 1)]

        for s in range(1, 5):
            for j in range(2):
                for g in range(2):
                    if (s, g, j) not in k:
                        continue
                    value = term(zo(sign[g] * (5 - s)), j)
                    if (s - 1, g, j) in k:
                        got(k[s - 1, g, j], rsr.at[it, s - 2, g, j])
                        value = value + rsr[it, s - 2, g, j].astype(F32)
                    rss[it, s - 1, g, j] = value.astype(BF16)
                    put(k[s, g, j], rss.at[it, s - 1, g, j], rsr.at[it, s - 1, g, j], dev(z_=zo(sign[g])))
        result = []
        for j in range(2):
            value = term(z, j)
            for g in range(2):
                got(k[4, g, j], rsr.at[it, 3, g, j])
                value = value + rsr[it, 3, g, j].astype(F32)
            result.append(value)
        return result

    def prefix(it, drift):
        ks = {i: next(ids) for i in (1, 2, 3)}
        for j in range(2):
            dsend[it, j] = drift[j].astype(BF16)
            pref[j] = jnp.zeros((T, W), F32)
        for i in (1, 2, 3):

            @pl.when(y + i < 4)
            def _(i=i):
                remote(dsend.at[it], drecv.at[it, i - 1], ks[i], ks[i], dev(y_=yo(i))).start()

        for i in (3, 2, 1):

            @pl.when(y - i >= 0)
            def _(i=i):
                got(ks[i], drecv.at[it, i - 1])
                for j in range(2):
                    pref[j] += drecv[it, i - 1, j].astype(F32)

        def done():
            for i in (1, 2, 3):

                @pl.when(y + i < 4)
                def _(i=i):
                    remote(dsend.at[it], drecv.at[it, i - 1], ks[i], ks[i], dev(y_=yo(i))).wait_send()

        return done

    swap_in(ks_state, sbuf)
    cur = [sbuf[j] for j in range(2)]
    k_stat = stats_send(0, cur)
    got(k_ms, mrecv.at[0])
    m1[...] = mbuf[...] + mrecv[0]
    k_ml = {k: next(ids) for k in (1, 2, 3)}
    for k in (1, 2, 3):
        put(k_ml[k], m1, mrecv.at[k], lo(k))
    for k in (1, 2, 3):
        got(k_ml[k], mrecv.at[k])
    m2[...] = m1[...] + mrecv[1] + mrecv[2] + mrecv[3]
    k_mx = {k: next(ids) for k in (1, 2, 3)}
    for k in (1, 2, 3):
        put(k_mx[k], m2, modall.at[x], dev(x_=xo(k)))
    modall[x] = m2[...]
    weight_far(0)
    for k in (1, 2, 3):
        got(k_mx[k], modall.at[xo(-k)])
    normalise(0, cur, k_stat)
    gather = Gather(0)
    gather.first()
    weight_near(0)
    gather.step(1)
    weight_far_x(0, 1)
    weight_far_x(0, 3)
    gather.step(2)
    weight_far(1)
    weight_far_x(0, 2)
    gather.step(3)
    weight_near(1)
    gather.step(4)
    weight_far_x(1, 1)
    weight_far_x(1, 3)
    weight_far_x(1, 2)
    gather.end()
    swap_in(ks_anchor, abuf)
    weight_end(0)
    first_matmul(0)
    weight_end(1)
    dones = []
    for it in range(ITERS):
        if it:
            cur = [abuf[j] + pref[j] for j in range(2)]
            k_stat = stats_send(it, cur)
            normalise(it, cur, k_stat)
            gather = Gather(it)
            gather.first()
            for s in range(1, 5):
                gather.step(s)
            gather.end()
            first_matmul(it)
        second_matmul(it)
        block = scatter(it)
        step = step_ref[0]
        drift = [step * mod(j, 2) * block[j] for j in range(2)]
        dones.append(prefix(it, drift))
    for j in range(2):
        fsend[j] = (pref[j] + drift[j]).astype(BF16)
    ks_out = swap_out(lambda j: fsend.at[j], frecv)
    swap_in(ks_out, frecv)
    for i in range(2):
        out_ref[T * i : T * (i + 1), :] = a_ref[T * i : T * (i + 1), :] + frecv[i].astype(F32)

    for copy in pending:
        copy.wait_send()
    for done in dones:
        done()
    for ks, src_of, dst in swaps:
        for i in range(2):

            @pl.when(jnp.logical_not(own[i]))
            def _(i=i):
                remote(src_of(i), dst.at[half], ks[i], ks[0] + half, swap[i]).wait_send()


def local(states, anchor, timesteps, step_sizes, weight_in, weight_out, mod_weight):
    embedding = timestep_embedding(timesteps)[0]
    rows_here = mod_weight.shape[0]
    embed_part = lax.dynamic_slice_in_dim(
        embedding, lax.axis_index("row") * rows_here, rows_here, 0
    )
    mod_part = jnp.einsum(
        "e,ekd->kd", embed_part, mod_weight.astype(jnp.float32), precision=lax.Precision.HIGHEST
    )
    vmem = pl.BlockSpec(memory_space=pltpu.VMEM)
    scratch = [
        pltpu.VMEM((2, T, W), F32),
        pltpu.VMEM((2, T, W), F32),
        pltpu.VMEM((8, W), F32),
        pltpu.VMEM((8, W), F32),
        pltpu.VMEM((8, W), F32),
        pltpu.VMEM((4, 8, W), F32),
        pltpu.VMEM((4, 8, W), F32),
        pltpu.VMEM((ITERS, T, 128), F32),
        pltpu.VMEM((ITERS, 3, T, 128), F32),
        pltpu.VMEM((ITERS, 4 * T, D), BF16),
        pltpu.VMEM((D, U), BF16),
        pltpu.VMEM((4, U, 2 * W), BF16),
        pltpu.VMEM((4 * T, U), BF16),
        pltpu.VMEM((ITERS, 2, 4 * T, 2 * W), BF16),
        pltpu.VMEM((ITERS, 2, 4 * T, 2 * W), BF16),
        pltpu.VMEM((2, 4, T, 2 * W), F32),
        pltpu.VMEM((ITERS, 4, 2, 2, T, W), BF16),
        pltpu.VMEM((ITERS, 4, 2, 2, T, W), BF16),
        pltpu.VMEM((ITERS, 2, T, W), BF16),
        pltpu.VMEM((ITERS, 3, 2, T, W), BF16),
        pltpu.VMEM((2, T, W), F32),
        pltpu.VMEM((2, T, W), BF16),
        pltpu.VMEM((2, T, W), BF16),
        pltpu.SemaphoreType.DMA((COPIES,)),
        pltpu.SemaphoreType.DMA((COPIES,)),
    ]
    out = pl.pallas_call(
        kernel,
        out_shape=jax.ShapeDtypeStruct(anchor.shape, F32),
        in_specs=[pl.BlockSpec(memory_space=pltpu.SMEM), vmem, vmem, vmem]
        + [pl.BlockSpec(memory_space=pl.ANY)] * 2,
        out_specs=vmem,
        scratch_shapes=scratch,
        compiler_params=pltpu.CompilerParams(
            collective_id=0, has_side_effects=True, vmem_limit_bytes=48 << 20
        ),
        name="picard",
    )(step_sizes, states[0], anchor, mod_part, weight_in, weight_out)
    return out[None]


def solution(mesh):
    placed = (
        P("tm", "row", "col"),
        P("row", "col"),
        P("tm"),
        P("tm"),
        P("col", "row"),
        P("row", "col"),
        P("row", None, "col"),
    )
    return jax.shard_map(
        local, mesh=mesh, in_specs=placed, out_specs=P("tm", "row", "col"), check_vma=False
    )
```

time: 685 us -> 186 us (0.27); the launches traced: 676 us -> 184 us
  waiting for transfers between devices: 493 us -> 0 us
  Pallas kernels: 0 us -> 177 us
  blocking collectives: 135 us -> 0 us
  matrix products: 20.4 us -> 0.46 us
  between operations: 15 us -> 1.4 us
  other arithmetic: 11.3 us -> 0.21 us
    reduce_scatter x4 -> x0, waiting for transfers between devices: 306 us -> none  [the longest x2 235 us: local(): lax.psum_scatter(jnp.dot(panels_all, weight_in, preferred_element_type=jn...]
    all_gather x2 -> x0, waiting for transfers between devices: 187 us -> none  [local(): hidden = lax.all_gather(hidden_share, 'col', axis=0, tiled=True)]
    pallas_call x0 -> x1, Pallas kernels: none -> 177 us  [local(): pl.pallas_call(kernel, out_shape=jax.ShapeDtypeStruct(anchor.shape, F32),...]
    psum x3 -> x0, blocking collectives: 72.1 us -> none  [the longest x2 57 us: local(): row_sum, squares = lax.psum((row_sum, squares), 'col')]
    all_gather x4 -> x0, blocking collectives: 63.3 us -> none  [the longest x2 45 us: local(): panels_all = lax.all_gather(normed, 'row', axis=0, tiled=True)]
    dot_general x4 -> x0, matrix products: 18.7 us -> none  [the longest x2 10.6 us: local(): jnp.dot(hidden, weight_out, preferred_element_type=jnp.float32)]
    convert_element_type x6 -> x0, other arithmetic: 7.36 us -> none  [the longest x2 4.31 us: local(): hidden_share = jax.nn.gelu(pre_share, approximate=True).astype(jnp.bfloat16)]
  transfers between devices with their start and end apart: 6 -> 0, of which waited for: 6 -> 0; matrix products, arithmetic and copies ran while one was open for 0% -> 0% of each run, Pallas kernels for 0% -> 0%
where the time goes in v1:
time: 186 us; the launch traced here: 184 us
  Pallas kernels  177 us (95%)
  local copies, waits for them, and re-layouts  5.14 us (3%)
    pallas_call x1, Pallas kernels, local(): pl.pallas_call(kernel, out_shape=jax.ShapeDtypeStruct(anchor.shape, F32),...  177 us
    unnamed x11, local copies, waits for them, and re-layouts  5.14 us

profile of v1, /device:TPU:17, one launch (start us, length us, event | category | flops | bytes accessed | tf_op | source)
XLA Modules:
  0.0 184.0 jit_solution(10915971262025542773)
XLA Ops:
  0.0 0.0 copy-start
  1.4 0.2 fusion
  1.6 0.0 copy-done
  1.6 0.5 fusion.3
  2.1 0.0 copy-start.1
  2.1 1.3 copy-done.1
  3.4 0.0 copy-start.2
  3.4 1.3 copy-done.2
  4.6 0.0 copy-start.3
  4.6 0.9 copy-done.3
  5.6 0.0 copy-start.4
  5.6 0.9 copy-done.4
  6.5 176.8 %picard.1 = f32[160,384]{1,0:T(8,128)S(1)} custom-call(f32[1]{0:T(128)S(6)} %copy.13.step_ref, f32[160,384]{1,0:T(8,128)S(1)} %bitcast.11, f32[160,384]{1,0:T(8,128)S(1)} %copy-done.4, f32[3,384]{1,0:T(4,128)S(1)} %bitcast.12, bf16[384,1536]{1,0:T(8,128)(2,1)S(1)} %copy-done.1, bf16[1536,384]{1,0:T(8,128)(2,1)S(1)} %copy-done.2), custom_call_target="tpu_custom_call" | custom-call | tf_op jit(solution)/shard_map/picard/pallas_call | solution.py:486
  183.3 0.7 copy.14
  (1 shorter events, 0.0 us)
Async XLA Ops:
  0.0 1.6 copy-start
  2.1 1.3 copy-start.1
  3.4 1.3 copy-start.2
  4.6 0.9 copy-start.3
  5.6 0.9 copy-start.4

commit v2 on v1

v2 whole, which is shorter than its diff:
```python
import math

import jax
import jax.numpy as jnp
from jax import lax
from jax.experimental import pallas as pl
from jax.experimental.pallas import tpu as pltpu
from jax.sharding import PartitionSpec as P

D = 3072
ITERS = 2
EPSILON = 1e-06
MESH = pl.DeviceIdType.MESH
F32 = jnp.float32
BF16 = jnp.bfloat16

T = 80
W = 384
U = 768

PARTS = ((0, 48), (48, 32))

COPIES = 304


def timestep_embedding(timesteps):
    half_width = D // 2
    positions = jnp.arange(half_width, dtype=jnp.float32)
    frequency = jnp.exp(-math.log(10000.0) * positions / half_width)
    phases = timesteps.astype(jnp.float32)[:, None] * frequency[None, :]
    return jnp.concatenate([jnp.cos(phases), jnp.sin(phases)], axis=1)


def kernel(
    step_ref, s_ref, a_ref, m_ref, wi_ref, wo_ref, out_ref,
    sbuf, abuf, mbuf, m1, m2, mrecv, modall, win, wout, pref, frecv,
    stat, statr, xall, hid, obs, obr, part, rss, rsr, dsend, drecv, fsend,
    send, recv,
):
    y = lax.axis_index("tm")
    row = lax.axis_index("row")
    col = lax.axis_index("col")
    l, c = row // 2, lax.rem(row, 2)
    h, x = col // 4, lax.rem(col, 4)
    z = 4 * h + l

    def dev(x_=None, y_=None, z_=None, c_=None):
        x_ = x if x_ is None else x_
        y_ = y if y_ is None else y_
        z_ = z if z_ is None else z_
        c_ = c if c_ is None else c_
        return (y_, 2 * lax.rem(z_, 4) + c_, 4 * (z_ // 4) + x_)

    def xo(k):
        return lax.rem(x + k + 4, 4)

    def yo(k):
        return lax.rem(y + k + 4, 4)

    def zo(k):
        return lax.rem(z + k + 8, 8)

    sib = dev(c_=1 - c)
    z4 = dev(z_=zo(4))
    z4sib = dev(z_=zo(4), c_=1 - c)

    def lo(k):
        return dev(z_=4 * h + lax.rem(l + k, 4))

    ids = iter(range(COPIES))
    pending = []

    def remote(src, dst, ss, rs, to):
        return pltpu.make_async_remote_copy(
            src_ref=src, dst_ref=dst, send_sem=send.at[ss], recv_sem=recv.at[rs],
            device_id=to, device_id_type=MESH,
        )

    def put(k, src, dst, to):
        copy = remote(src, dst, k, k, to)
        copy.start()
        pending.append(copy)

    def got(k, dst):
        remote(dst, dst, k, k, sib).wait_recv()

    partners = [sib, z4, z4sib, dev(z_=zo(1)), dev(z_=zo(-1))]
    partners += [dev(x_=xo(k)) for k in (1, 2, 3)]
    partners += [dev(y_=yo(k)) for k in (1, 2, 3)]
    partners += [lo(k) for k in (1, 2, 3)]
    barrier = pltpu.get_barrier_semaphore()
    for p in partners:
        pl.semaphore_signal(barrier, inc=1, device_id=p, device_id_type=MESH)
    half = lax.rem(x, 2)
    same = x // 2 == c
    swap = [dev(x_=2 * c + i, c_=x // 2) for i in range(2)]
    swap_y = {(i, k): dev(x_=2 * c + i, c_=x // 2, y_=yo(k)) for i in range(2) for k in (1, 2, 3)}
    for p in swap_y.values():
        pl.semaphore_signal(barrier, inc=1, device_id=p, device_id_type=MESH)
    own = [jnp.logical_and(same, half == i) for i in range(2)]
    for i in range(2):

        @pl.when(jnp.logical_not(own[i]))
        def _(i=i):
            pl.semaphore_signal(barrier, inc=1, device_id=swap[i], device_id_type=MESH)

    pl.semaphore_wait(barrier, len(partners) + len(swap_y) + 2 - same.astype(jnp.int32))

    swaps = []

    def swap_out(src_of, dst):
        ks = (next(ids), next(ids))
        for i in range(2):

            @pl.when(own[i])
            def _(i=i):
                pltpu.make_async_copy(src_of(i), dst.at[half], recv.at[ks[0] + half]).start()

            @pl.when(jnp.logical_not(own[i]))
            def _(i=i):
                remote(src_of(i), dst.at[half], ks[i], ks[0] + half, swap[i]).start()

        swaps.append((ks, src_of, dst))
        return ks

    def swap_in(ks, dst):
        for i in range(2):
            got(ks[i], dst.at[i])

    ks_state = swap_out(lambda i: s_ref.at[pl.ds(T * i, T)], sbuf)

    mbuf[...] = jnp.zeros_like(mbuf)
    mbuf[0:3, :] = m_ref[...]
    k_ms = next(ids)
    put(k_ms, mbuf, mrecv.at[0], sib)

    mine = 4 * h + x
    far = 4 * (1 - h)

    def win_slot(hx, first=0, rows=W):
        return win.at[pl.ds(pl.multiple_of(hx * W + first, 16), rows), :]

    def wout_slot(hx, first=0, rows=U):
        return wout.at[
            hx // 2, pl.ds(pl.multiple_of(first, 16), rows), pl.ds(pl.multiple_of(lax.rem(hx, 2) * W, 128), W)
        ]

    def wi_part(hd, first, rows):
        return wi_ref.at[pl.ds(pl.multiple_of(first, 16), rows), pl.ds(pl.multiple_of(hd * U, 128), U)]

    def wo_part(hd, first, rows):
        return wo_ref.at[pl.ds(pl.multiple_of(hd * U + first, 16), rows), :]

    sides = ((wi_part, win_slot, W), (wo_part, wout_slot, U))
    ids_w = []
    local = [None, None]
    for part_of, slot_of, rows in sides:
        k_x = {k: next(ids) for k in (1, 3)}
        k_fwd = {k: next(ids) for k in (1, 3)}
        k_z = next(ids)
        k_xq = {k: next(ids) for k in (1, 2, 3)}
        k_y = {(s, k, f): next(ids) for s in range(4) for k in (1, 3) for f in range(2)}
        k_own = next(ids)
        ids_w.append((k_x, k_fwd, k_z, k_xq, k_y, k_own))

    def far_start(w):
        part_of, slot_of, rows = sides[w]
        k_x, k_fwd, k_z, k_xq, k_y, k_own = ids_w[w]
        q = rows // 4
        put(k_z, part_of(1 - h, y * q, q), slot_of(mine, y * q, q), z4)

    def near_start(w):
        part_of, slot_of, rows = sides[w]
        k_x, k_fwd, k_z, k_xq, k_y, k_own = ids_w[w]
        for k in (1, 3):
            put(k_x[k], part_of(h, 0, rows), slot_of(mine), dev(x_=xo(k)))
        copy = pltpu.make_async_copy(part_of(h, 0, rows), slot_of(mine), recv.at[k_own])
        copy.start()
        local[w] = copy

    def weight_far(w):
        part_of, slot_of, rows = sides[w]
        k_x, k_fwd, k_z, k_xq, k_y, k_own = ids_w[w]
        q = rows // 4
        here = slot_of(far + x, y * q, q)
        got(k_z, here)
        for k in (2, 1, 3):
            put(k_xq[k], here, here, dev(x_=xo(k)))
        for k in (1, 3):
            put(k_y[0, k, 0], here, here, dev(y_=yo(k)))

    def weight_far_x(w, s):
        part_of, slot_of, rows = sides[w]
        k_x, k_fwd, k_z, k_xq, k_y, k_own = ids_w[w]
        q = rows // 4
        here = slot_of(far + xo(-s), y * q, q)
        got(k_xq[s], here)
        for k in (1, 3):
            put(k_y[s, k, 0], here, here, dev(y_=yo(k)))

    def weight_far_y(w, s):
        part_of, slot_of, rows = sides[w]
        k_x, k_fwd, k_z, k_xq, k_y, k_own = ids_w[w]
        q = rows // 4
        for k, first in ((1, 0), (3, q // 2)):
            got(k_y[s, k, 0], slot_of(far + xo(-s), yo(-k) * q, q))
            there = slot_of(far + xo(-s), yo(-k) * q + first, q // 2)
            put(k_y[s, k, 1], there, there, dev(y_=yo(k)))

    def weight_near(w):
        part_of, slot_of, rows = sides[w]
        k_x, k_fwd, k_z, k_xq, k_y, k_own = ids_w[w]
        for k, first in ((1, 0), (3, rows // 2)):
            got(k_x[k], slot_of(4 * h + xo(-k)))
            there = slot_of(4 * h + xo(-k), first, rows // 2)
            put(k_fwd[k], there, there, dev(x_=xo(k)))

    def weight_end(w):
        part_of, slot_of, rows = sides[w]
        k_x, k_fwd, k_z, k_xq, k_y, k_own = ids_w[w]
        q = rows // 4
        for k, first in ((1, 0), (3, rows // 2)):
            got(k_fwd[k], slot_of(4 * h + xo(2), first, rows // 2))
        for s in range(4):
            for k, first in ((1, 0), (3, q // 2)):
                got(k_y[s, k, 1], slot_of(far + xo(-s), yo(2) * q + first, q // 2))
        local[w].wait()

    far_start(0)
    far_start(1)
    near_start(0)
    ks_anchor = swap_out(lambda i: a_ref.at[pl.ds(T * i, T)], abuf)

    def mod(j, r):
        return modall[2 * c + j, r : r + 1, :]

    sign = (1, -1)

    class Part:
        def __init__(self, it, p):
            self.it, self.p = it, p
            self.first, self.n = PARTS[p]
            self.x, self.hid, self.part = xall[p].at[it], hid[p], part[p]
            self.k_stat = [next(ids) for _ in range(3)]
            steps = [(s, g, j) for s in range(1, 5) for j in range(2) for g in range(2)]
            self.k_ring = {key: next(ids) for key in steps if key[0] < 4 or key[1] == key[2]}
            self.k_sib = {key: next(ids) for key in self.k_ring}
            self.k_own = [next(ids) for _ in range(2)]
            self.k_half = [next(ids) for _ in range(2)]
            self.k_sum = {key: next(ids) for key in steps if key[0] > 1 or key[1] == key[2]}
            self.k_prefix = {i: next(ids) for i in (1, 2, 3)}

        def rows(self):
            return slice(self.first, self.first + self.n)

        def stats(self, cur):
            self.cur = cur
            own, there = stat[self.p].at[self.it], statr[self.p].at[self.it]
            total = sum(jnp.sum(v, axis=1, keepdims=True) for v in cur)
            squares = sum(jnp.sum(v * v, axis=1, keepdims=True) for v in cur)
            lane = lax.broadcasted_iota(jnp.int32, (self.n, 128), 1)
            own[...] = jnp.where(lane < 64, total, squares)
            for i, to in enumerate((z4, z4sib, sib)):
                put(self.k_stat[i], own, there.at[i], to)

        def slot(self, zz, cc, j):
            hh, ll = zz // 4, lax.rem(zz, 4)
            return self.x.at[
                pl.ds(pl.multiple_of(ll * self.n, 16), self.n),
                pl.ds(pl.multiple_of((4 * hh + 2 * cc + j) * W, 128), W),
            ]

        def normalise(self):
            own, there = stat[self.p].at[self.it], statr[self.p].at[self.it]
            for i, k in enumerate(self.k_stat):
                got(k, there.at[i])
            total = own[...] + there[0] + there[1] + there[2]
            mean = total[:, 0:1] / D
            var = total[:, 64:65] / D - mean * mean
            scale = lax.rsqrt(var + EPSILON)
            for j in range(2):
                value = (self.cur[j] - mean) * scale * (1.0 + mod(j, 1)) + mod(j, 0)
                slot = self.slot(z, c, j)
                slot[...] = value.astype(BF16)
                for g in range(2):
                    put(self.k_ring[1, g, j], slot, slot, dev(z_=zo(sign[g])))
                put(self.k_own[j], slot, slot, sib)

        def gather(self, s):
            for j in range(2):
                for g in range(2):
                    if (s, g, j) not in self.k_ring:
                        continue
                    slot = self.slot(zo(-sign[g] * s), c, j)
                    got(self.k_ring[s, g, j], slot)
                    if (s + 1, g, j) in self.k_ring:
                        put(self.k_ring[s + 1, g, j], slot, slot, dev(z_=zo(sign[g])))
                    put(self.k_sib[s, g, j], slot, slot, sib)

        def gathered(self):
            for j in range(2):
                got(self.k_own[j], self.slot(z, 1 - c, j))
            for (s, g, j), k in self.k_sib.items():
                got(k, self.slot(zo(-sign[g] * s), 1 - c, j))

        def first_matmul(self):
            def tile(n, _):
                cols = pl.ds(pl.multiple_of(n * 256, 256), 256)
                pre = jnp.dot(self.x[...], win[:, cols], preferred_element_type=F32)
                self.hid[:, cols] = jax.nn.gelu(pre, approximate=True).astype(BF16)
                return 0

            lax.fori_loop(0, U // 256, tile, 0)

        def second_other(self):
            there, back = obs[self.p].at[self.it], obr[self.p].at[self.it]
            for hh in range(2):

                def tile(n, _, hh=hh):
                    cols = pl.ds(pl.multiple_of(n * 256, 256), 256)
                    other = jnp.dot(self.hid[...], wout[2 * hh + 1 - c, :, cols], preferred_element_type=F32)
                    there[hh, :, cols] = other.astype(BF16)
                    return 0

                lax.fori_loop(0, 3, tile, 0)
                put(self.k_half[hh], there.at[hh], back.at[hh], sib)

        def second_own(self):
            for hh in range(2):

                def tile(n, _, hh=hh):
                    cols = pl.ds(pl.multiple_of(n * 256, 256), 256)
                    kept = jnp.dot(self.hid[...], wout[2 * hh + c, :, cols], preferred_element_type=F32)
                    self.part[hh, :, :, cols] = kept.reshape(4, self.n, 256)
                    return 0

                lax.fori_loop(0, 3, tile, 0)

        def halves(self):
            back = obr[self.p].at[self.it]
            for hh in range(2):
                got(self.k_half[hh], back.at[hh])
                self.part[hh] += back[hh].astype(F32).reshape(4, self.n, 2 * W)

        def term(self, d, j):
            return self.part[d // 4, lax.rem(d, 4), :, W * j : W * (j + 1)]

        def scatter(self, s):
            out, back = rss[self.p].at[self.it], rsr[self.p].at[self.it]
            for j in range(2):
                for g in range(2):
                    if (s, g, j) not in self.k_sum:
                        continue
                    value = self.term(zo(sign[g] * (5 - s)), j)
                    if (s - 1, g, j) in self.k_sum:
                        got(self.k_sum[s - 1, g, j], back.at[s - 2, g, j])
                        value = value + back[s - 2, g, j].astype(F32)
                    out[s - 1, g, j] = value.astype(BF16)
                    put(self.k_sum[s, g, j], out.at[s - 1, g, j], back.at[s - 1, g, j], dev(z_=zo(sign[g])))

        def scattered(self):
            back = rsr[self.p].at[self.it]
            self.drift = []
            for j in range(2):
                value = self.term(z, j)
                for g in range(2):
                    got(self.k_sum[4, g, j], back.at[3, g, j])
                    value = value + back[3, g, j].astype(F32)
                self.drift.append(step_ref[0] * mod(j, 2) * value)

        def prefix_copy(self, i):
            return remote(
                dsend[self.p], drecv[self.p].at[i - 1], self.k_prefix[i], self.k_prefix[i], dev(y_=yo(i))
            )

        def prefix_send(self):
            for j in range(2):
                dsend[self.p][j] = self.drift[j].astype(BF16)
            for i in (1, 2, 3):

                @pl.when(y + i < 4)
                def _(i=i):
                    self.prefix_copy(i).start()

        def prefix_add(self):
            pref[:, self.rows(), :] = jnp.zeros((2, self.n, W), F32)
            for i in (3, 2, 1):

                @pl.when(y - i >= 0)
                def _(i=i):
                    got(self.k_prefix[i], drecv[self.p].at[i - 1])
                    for j in range(2):
                        pref[j, self.rows(), :] += drecv[self.p][i - 1, j].astype(F32)

        def prefix_sent(self):
            for i in (1, 2, 3):

                @pl.when(y + i < 4)
                def _(i=i):
                    self.prefix_copy(i).wait_send()

        def current(self):
            return [abuf[j, self.rows(), :] + pref[j, self.rows(), :] for j in range(2)]

        def out_copy(self, k, i):
            there = frecv.at[k, half, pl.ds(self.first, self.n)]
            to = swap[i] if k == 0 else swap_y[i, k]
            return remote(fsend[self.p].at[i], there, self.k_out[k, i], self.k_out[k, 0] + half, to)

        def out_send(self):
            self.k_out = {(k, i): next(ids) for k in range(4) for i in range(2)}
            for i in range(2):
                fsend[self.p][i] = self.drift[i].astype(BF16)
            for k in (3, 2, 1, 0):
                for i in range(2):
                    if k:

                        @pl.when(y + k < 4)
                        def _(i=i, k=k):
                            self.out_copy(k, i).start()

                    else:
                        there = frecv.at[0, half, pl.ds(self.first, self.n)]

                        @pl.when(own[i])
                        def _(i=i):
                            pltpu.make_async_copy(
                                fsend[self.p].at[i], there, recv.at[self.k_out[0, 0] + half]
                            ).start()

                        @pl.when(jnp.logical_not(own[i]))
                        def _(i=i):
                            self.out_copy(0, i).start()

        def out_sent(self):
            for k in range(4):
                for i in range(2):

                    @pl.when(y + k < 4 if k else jnp.logical_not(own[i]))
                    def _(i=i, k=k):
                        self.out_copy(k, i).wait_send()

        def out_add(self):
            for i in range(2):
                rows = slice(T * i + self.first, T * i + self.first + self.n)
                out_ref[rows, :] = a_ref[rows, :]
                for k in (3, 2, 1, 0):

                    @pl.when(y - k >= 0)
                    def _(i=i, k=k):
                        got(self.k_out[k, i], frecv.at[k, i, pl.ds(self.first, self.n)])
                        out_ref[rows, :] += frecv[k, i, self.rows(), :].astype(F32)

    parts = [[Part(it, p) for p in range(2)] for it in range(ITERS)]
    a, b = parts[0]

    swap_in(ks_state, sbuf)
    for v in (a, b):
        v.stats([sbuf[j, v.rows(), :] for j in range(2)])
    got(k_ms, mrecv.at[0])
    m1[...] = mbuf[...] + mrecv[0]
    k_ml = {k: next(ids) for k in (1, 2, 3)}
    for k in (1, 2, 3):
        put(k_ml[k], m1, mrecv.at[k], lo(k))
    weight_far(0)
    for k in (1, 2, 3):
        got(k_ml[k], mrecv.at[k])
    m2[...] = m1[...] + mrecv[1] + mrecv[2] + mrecv[3]
    k_mx = {k: next(ids) for k in (1, 2, 3)}
    for k in (1, 2, 3):
        put(k_mx[k], m2, modall.at[x], dev(x_=xo(k)))
    modall[x] = m2[...]
    weight_far(1)
    near_start(1)
    for k in (1, 2, 3):
        got(k_mx[k], modall.at[xo(-k)])
    for v in (a, b):
        v.normalise()
    weight_near(0)
    weight_far_y(0, 0)
    for v in (a, b):
        v.gather(1)
    weight_far_x(0, 1)
    weight_far_x(0, 3)
    weight_far_y(1, 0)
    for v in (a, b):
        v.gather(2)
    weight_far_x(0, 2)
    weight_far_x(1, 1)
    weight_far_x(1, 3)
    weight_far_y(0, 1)
    for v in (a, b):
        v.gather(3)
    weight_far_y(0, 3)
    weight_far_x(1, 2)
    weight_far_y(0, 2)
    for v in (a, b):
        v.gather(4)
    weight_near(1)
    weight_far_y(1, 1)
    weight_far_y(1, 3)
    swap_in(ks_anchor, abuf)
    a.gathered()
    b.gathered()
    weight_far_y(1, 2)
    weight_end(0)
    a.first_matmul()
    b.first_matmul()
    weight_end(1)
    for it in range(ITERS):
        a, b = parts[it]
        if it:
            a.gathered()
            a.first_matmul()
        a.second_other()
        a.second_own()
        if it:
            b.gather(4)
            b.gathered()
        a.halves()
        a.scatter(1)
        if it:
            b.first_matmul()
        b.second_other()
        a.scatter(2)
        b.second_own()
        b.halves()
        b.scatter(1)
        a.scatter(3)
        b.scatter(2)
        a.scatter(4)
        b.scatter(3)
        a.scattered()
        if it + 1 == ITERS:
            a.out_send()
            b.scatter(4)
            b.scattered()
            b.out_send()
            a.out_add()
            b.out_add()
            continue
        a.prefix_send()
        b.scatter(4)
        b.scattered()
        b.prefix_send()
        c1, d1 = parts[it + 1]
        a.prefix_add()
        c1.stats(a.current())
        b.prefix_add()
        d1.stats(b.current())
        c1.normalise()
        d1.normalise()
        for s in range(1, 4):
            c1.gather(s)
            d1.gather(s)
        c1.gather(4)

    for copy in pending:
        copy.wait_send()
    for v in parts[0]:
        v.prefix_sent()
    for v in parts[1]:
        v.out_sent()
    for ks, src_of, dst in swaps:
        for i in range(2):

            @pl.when(jnp.logical_not(own[i]))
            def _(i=i):
                remote(src_of(i), dst.at[half], ks[i], ks[0] + half, swap[i]).wait_send()


def local(states, anchor, timesteps, step_sizes, weight_in, weight_out, mod_weight):
    embedding = timestep_embedding(timesteps)[0]
    rows_here = mod_weight.shape[0]
    embed_part = lax.dynamic_slice_in_dim(
        embedding, lax.axis_index("row") * rows_here, rows_here, 0
    )
    mod_part = jnp.einsum(
        "e,ekd->kd", embed_part, mod_weight.astype(jnp.float32), precision=lax.Precision.HIGHEST
    )
    vmem = pl.BlockSpec(memory_space=pltpu.VMEM)

    def each(make):
        return [make(n) for _, n in PARTS]

    scratch = [
        pltpu.VMEM((2, T, W), F32),
        pltpu.VMEM((2, T, W), F32),
        pltpu.VMEM((8, W), F32),
        pltpu.VMEM((8, W), F32),
        pltpu.VMEM((8, W), F32),
        pltpu.VMEM((4, 8, W), F32),
        pltpu.VMEM((4, 8, W), F32),
        pltpu.VMEM((D, U), BF16),
        pltpu.VMEM((4, U, 2 * W), BF16),
        pltpu.VMEM((2, T, W), F32),
        pltpu.VMEM((4, 2, T, W), BF16),
        each(lambda n: pltpu.VMEM((ITERS, n, 128), F32)),
        each(lambda n: pltpu.VMEM((ITERS, 3, n, 128), F32)),
        each(lambda n: pltpu.VMEM((ITERS, 4 * n, D), BF16)),
        each(lambda n: pltpu.VMEM((4 * n, U), BF16)),
        each(lambda n: pltpu.VMEM((ITERS, 2, 4 * n, 2 * W), BF16)),
        each(lambda n: pltpu.VMEM((ITERS, 2, 4 * n, 2 * W), BF16)),
        each(lambda n: pltpu.VMEM((2, 4, n, 2 * W), F32)),
        each(lambda n: pltpu.VMEM((ITERS, 4, 2, 2, n, W), BF16)),
        each(lambda n: pltpu.VMEM((ITERS, 4, 2, 2, n, W), BF16)),
        each(lambda n: pltpu.VMEM((2, n, W), BF16)),
        each(lambda n: pltpu.VMEM((3, 2, n, W), BF16)),
        each(lambda n: pltpu.VMEM((2, n, W), BF16)),
        pltpu.SemaphoreType.DMA((COPIES,)),
        pltpu.SemaphoreType.DMA((COPIES,)),
    ]
    out = pl.pallas_call(
        kernel,
        out_shape=jax.ShapeDtypeStruct(anchor.shape, F32),
        in_specs=[pl.BlockSpec(memory_space=pltpu.SMEM), vmem, vmem, vmem]
        + [pl.BlockSpec(memory_space=pl.ANY)] * 2,
        out_specs=vmem,
        scratch_shapes=scratch,
        compiler_params=pltpu.CompilerParams(
            collective_id=0, has_side_effects=True, vmem_limit_bytes=60 << 20
        ),
        name="picard",
    )(step_sizes, states[0], anchor, mod_part, weight_in, weight_out)
    return out[None]


def solution(mesh):
    placed = (
        P("tm", "row", "col"),
        P("row", "col"),
        P("tm"),
        P("tm"),
        P("col", "row"),
        P("row", "col"),
        P("row", None, "col"),
    )
    return jax.shard_map(
        local, mesh=mesh, in_specs=placed, out_specs=P("tm", "row", "col"), check_vma=False
    )
```

time: 186 us -> 161 us (0.87)
  Pallas kernels: 177 us -> 156 us
  local copies, waits for them, and re-layouts: 5.14 us -> 2.27 us
    pallas_call x1, Pallas kernels: 177 us -> 156 us  [local(): pl.pallas_call(kernel, out_shape=jax.ShapeDtypeStruct(anchor.shape, F32),...]
    unnamed x11 -> x3, local copies, waits for them, and re-layouts: 5.14 us -> 1.66 us
where the time goes in v2:
time: 161 us; the launch traced here: 160 us
  Pallas kernels  156 us (97%)
  local copies, waits for them, and re-layouts  2.27 us (1%)
    pallas_call x1, Pallas kernels, local(): pl.pallas_call(kernel, out_shape=jax.ShapeDtypeStruct(anchor.shape, F32),...  156 us

profile of v2, /device:TPU:17, one launch (start us, length us, event | category | flops | bytes accessed | tf_op | source)
XLA Modules:
  0.0 159.9 jit_solution(11176327456245801554)
XLA Ops:
  0.0 0.0 copy-start
  1.4 0.2 fusion
  1.6 0.0 copy-done
  1.6 0.5 fusion.3
  2.1 0.6 copy.10
  2.7 155.6 %picard.1 = f32[160,384]{1,0:T(8,128)} custom-call(f32[1]{0:T(128)S(6)} %copy.13.step_ref, f32[160,384]{1,0:T(8,128)} %bitcast.11, f32[160,384]{1,0:T(8,128)} %a_ref.1, f32[3,384]{1,0:T(4,128)} %bitcast.12, bf16[384,1536]{1,0:T(8,128)(2,1)} %wi_ref.1, bf16[1536,384]{1,0:T(8,128)(2,1)} %wo_ref.1), custom_call_target="tpu_custom_call" | custom-call | tf_op jit(solution)/shard_map/picard/pallas_call | solution.py:613
  158.3 1.7 %copy.14 = f32[1,160,384]{2,1,0:T(8,128)} copy(f32[1,160,384]{2,1,0:T(8,128)} %bitcast.10) | data formatting | bytes 491520
Async XLA Ops:
  0.0 1.6 copy-start

commit v3 on v2

--- a/solution.py
+++ b/solution.py
@@ -20,7 +20,8 @@
 
 PARTS = ((0, 48), (48, 32))
 
-COPIES = 304
+UNITS = ((0, 256), (256, 128))
+COPIES = 400
 
 
 def timestep_embedding(timesteps):
@@ -34,7 +35,7 @@
 def kernel(
     step_ref, s_ref, a_ref, m_ref, wi_ref, wo_ref, out_ref,
     sbuf, abuf, mbuf, m1, m2, mrecv, modall, win, wout, pref, frecv,
-    stat, statr, xall, hid, obs, obr, part, rss, rsr, dsend, drecv, fsend,
+    stat, statr, xall, hid, obs, obr, part, rss, rsr, dsend, drecv, fsend, drift,
     send, recv,
 ):
     y = lax.axis_index("tm")
@@ -137,99 +138,84 @@
     mine = 4 * h + x
     far = 4 * (1 - h)
 
-    def win_slot(hx, first=0, rows=W):
-        return win.at[pl.ds(pl.multiple_of(hx * W + first, 16), rows), :]
-
-    def wout_slot(hx, first=0, rows=U):
-        return wout.at[
-            hx // 2, pl.ds(pl.multiple_of(first, 16), rows), pl.ds(pl.multiple_of(lax.rem(hx, 2) * W, 128), W)
-        ]
-
-    def wi_part(hd, first, rows):
-        return wi_ref.at[pl.ds(pl.multiple_of(first, 16), rows), pl.ds(pl.multiple_of(hd * U, 128), U)]
-
-    def wo_part(hd, first, rows):
-        return wo_ref.at[pl.ds(pl.multiple_of(hd * U + first, 16), rows), :]
-
-    sides = ((wi_part, win_slot, W), (wo_part, wout_slot, U))
-    ids_w = []
-    local = [None, None]
-    for part_of, slot_of, rows in sides:
-        k_x = {k: next(ids) for k in (1, 3)}
-        k_fwd = {k: next(ids) for k in (1, 3)}
-        k_z = next(ids)
-        k_xq = {k: next(ids) for k in (1, 2, 3)}
-        k_y = {(s, k, f): next(ids) for s in range(4) for k in (1, 3) for f in range(2)}
-        k_own = next(ids)
-        ids_w.append((k_x, k_fwd, k_z, k_xq, k_y, k_own))
-
-    def far_start(w):
-        part_of, slot_of, rows = sides[w]
-        k_x, k_fwd, k_z, k_xq, k_y, k_own = ids_w[w]
-        q = rows // 4
-        put(k_z, part_of(1 - h, y * q, q), slot_of(mine, y * q, q), z4)
-
-    def near_start(w):
-        part_of, slot_of, rows = sides[w]
-        k_x, k_fwd, k_z, k_xq, k_y, k_own = ids_w[w]
-        for k in (1, 3):
-            put(k_x[k], part_of(h, 0, rows), slot_of(mine), dev(x_=xo(k)))
-        copy = pltpu.make_async_copy(part_of(h, 0, rows), slot_of(mine), recv.at[k_own])
-        copy.start()
-        local[w] = copy
-
-    def weight_far(w):
-        part_of, slot_of, rows = sides[w]
-        k_x, k_fwd, k_z, k_xq, k_y, k_own = ids_w[w]
-        q = rows // 4
-        here = slot_of(far + x, y * q, q)
-        got(k_z, here)
-        for k in (2, 1, 3):
-            put(k_xq[k], here, here, dev(x_=xo(k)))
-        for k in (1, 3):
-            put(k_y[0, k, 0], here, here, dev(y_=yo(k)))
-
-    def weight_far_x(w, s):
-        part_of, slot_of, rows = sides[w]
-        k_x, k_fwd, k_z, k_xq, k_y, k_own = ids_w[w]
-        q = rows // 4
-        here = slot_of(far + xo(-s), y * q, q)
-        got(k_xq[s], here)
-        for k in (1, 3):
-            put(k_y[s, k, 0], here, here, dev(y_=yo(k)))
-
-    def weight_far_y(w, s):
-        part_of, slot_of, rows = sides[w]
-        k_x, k_fwd, k_z, k_xq, k_y, k_own = ids_w[w]
-        q = rows // 4
-        for k, first in ((1, 0), (3, q // 2)):
-            got(k_y[s, k, 0], slot_of(far + xo(-s), yo(-k) * q, q))
-            there = slot_of(far + xo(-s), yo(-k) * q + first, q // 2)
-            put(k_y[s, k, 1], there, there, dev(y_=yo(k)))
-
-    def weight_near(w):
-        part_of, slot_of, rows = sides[w]
-        k_x, k_fwd, k_z, k_xq, k_y, k_own = ids_w[w]
-        for k, first in ((1, 0), (3, rows // 2)):
-            got(k_x[k], slot_of(4 * h + xo(-k)))
-            there = slot_of(4 * h + xo(-k), first, rows // 2)
-            put(k_fwd[k], there, there, dev(x_=xo(k)))
-
-    def weight_end(w):
-        part_of, slot_of, rows = sides[w]
-        k_x, k_fwd, k_z, k_xq, k_y, k_own = ids_w[w]
-        q = rows // 4
-        for k, first in ((1, 0), (3, rows // 2)):
-            got(k_fwd[k], slot_of(4 * h + xo(2), first, rows // 2))
-        for s in range(4):
-            for k, first in ((1, 0), (3, q // 2)):
-                got(k_y[s, k, 1], slot_of(far + xo(-s), yo(2) * q + first, q // 2))
-        local[w].wait()
-
-    far_start(0)
-    far_start(1)
-    near_start(0)
-    ks_anchor = swap_out(lambda i: a_ref.at[pl.ds(T * i, T)], abuf)
+    def win_side():
+        def slot_of(hx, first=0, rows=W):
+            return win.at[pl.ds(pl.multiple_of(hx * W + first, 16), rows), :]
+
+        def part_of(hd, first, rows):
+            return wi_ref.at[pl.ds(pl.multiple_of(first, 16), rows), pl.ds(pl.multiple_of(hd * U, 128), U)]
+
+        return part_of, slot_of, W
+
+    def wout_side(col, cols):
+        def slot_of(hx, first=0, rows=U):
+            return wout.at[
+                hx // 2,
+                pl.ds(pl.multiple_of(first, 16), rows),
+                pl.ds(pl.multiple_of(lax.rem(hx, 2) * W + col, 128), cols),
+            ]
+
+        def part_of(hd, first, rows):
+            return wo_ref.at[pl.ds(pl.multiple_of(hd * U + first, 16), rows), col : col + cols]
+
+        return part_of, slot_of, U
+
+    class Side:
+        def __init__(self, part_of, slot_of, rows):
+            self.part_of, self.slot_of, self.rows, self.q = part_of, slot_of, rows, rows // 4
+            self.k_x = {k: next(ids) for k in (1, 3)}
+            self.k_in = [next(ids) for _ in range(5)]
+            self.k_y = {(s, k, f): next(ids) for s in range(5) for k in (1, 3) for f in range(2)}
+            self.k_own = next(ids)
+
+        def quarter(self, s, yy, first=0, rows=None):
+            hx = 4 * h + xo(2) if s == 4 else far + xo(-s)
+            return self.slot_of(hx, yy * self.q + first, rows or self.q)
+
+        def far_start(self):
+            put(self.k_in[0], self.part_of(1 - h, y * self.q, self.q), self.slot_of(mine, y * self.q, self.q), z4)
+
+        def cross_start(self):
+            to = dev(x_=xo(2))
+            put(self.k_in[4], self.part_of(h, y * self.q, self.q), self.slot_of(mine, y * self.q, self.q), to)
+
+        def near_start(self):
+            for k in (1, 3):
+                put(self.k_x[k], self.part_of(h, 0, self.rows), self.slot_of(mine), dev(x_=xo(k)))
+            self.copy = pltpu.make_async_copy(self.part_of(h, 0, self.rows), self.slot_of(mine), recv.at[self.k_own])
+            self.copy.start()
+
+        def arrive(self, s):
+            here = self.quarter(s, y)
+            got(self.k_in[s], here)
+            if s == 0:
+                for k in (2, 1, 3):
+                    put(self.k_in[k], here, here, dev(x_=xo(k)))
+            for k in (1, 3):
+                put(self.k_y[s, k, 0], here, here, dev(y_=yo(k)))
+
+        def spread(self, s):
+            for k, first in ((1, 0), (3, self.q // 2)):
+                got(self.k_y[s, k, 0], self.quarter(s, yo(-k)))
+                there = self.quarter(s, yo(-k), first, self.q // 2)
+                put(self.k_y[s, k, 1], there, there, dev(y_=yo(k)))
+
+        def end(self):
+            for k in (1, 3):
+                got(self.k_x[k], self.slot_of(4 * h + xo(-k)))
+            for s in range(5):
+                for k, first in ((1, 0), (3, self.q // 2)):
+                    got(self.k_y[s, k, 1], self.quarter(s, yo(2), first, self.q // 2))
+            self.copy.wait()
+
+    w_in = Side(*win_side())
+    w_a, w_b = (Side(*wout_side(*unit)) for unit in UNITS)
+    w_in.cross_start()
+    w_in.far_start()
+    w_in.near_start()
+    w_a.far_start()
+    w_a.cross_start()
+    w_b.far_start()
 
     def mod(j, r):
         return modall[2 * c + j, r : r + 1, :]
@@ -246,8 +232,11 @@
             self.k_ring = {key: next(ids) for key in steps if key[0] < 4 or key[1] == key[2]}
             self.k_sib = {key: next(ids) for key in self.k_ring}
             self.k_own = [next(ids) for _ in range(2)]
-            self.k_half = [next(ids) for _ in range(2)]
-            self.k_sum = {key: next(ids) for key in steps if key[0] > 1 or key[1] == key[2]}
+            self.units = ((0, W),) if it else UNITS
+            self.k_half = {(u, hh): next(ids) for u in self.units for hh in range(2)}
+            self.k_sum = {
+                u: {key: next(ids) for key in steps if key[0] > 1 or key[1] == key[2]} for u in self.units
+            }
             self.k_prefix = {i: next(ids) for i in (1, 2, 3)}
 
         def rows(self):
@@ -312,61 +301,69 @@
 
             lax.fori_loop(0, U // 256, tile, 0)
 
-        def second_other(self):
+        def tiles(self, u):
+            if u[1] < W:
+                return [(j, u[0], u[1]) for j in range(2)]
+            return [(None, 256 * n, 256) for n in range(3)]
+
+        def second(self, cc, hh, u):
+            for j, col, cols in self.tiles(u):
+                at = col if j is None else W * j + col
+                yield at, cols, jnp.dot(self.hid[...], wout[2 * hh + cc, :, at : at + cols], preferred_element_type=F32)
+
+        def second_other(self, u):
             there, back = obs[self.p].at[self.it], obr[self.p].at[self.it]
             for hh in range(2):
-
-                def tile(n, _, hh=hh):
-                    cols = pl.ds(pl.multiple_of(n * 256, 256), 256)
-                    other = jnp.dot(self.hid[...], wout[2 * hh + 1 - c, :, cols], preferred_element_type=F32)
-                    there[hh, :, cols] = other.astype(BF16)
-                    return 0
-
-                lax.fori_loop(0, 3, tile, 0)
-                put(self.k_half[hh], there.at[hh], back.at[hh], sib)
-
-        def second_own(self):
+                for at, cols, value in self.second(1 - c, hh, u):
+                    for j, col in ((n // 3, n % 3 * 128) for n in range(at // 128, (at + cols) // 128)):
+                        first = W * j + col - at
+                        there[hh, j, :, col : col + 128] = value[:, first : first + 128].astype(BF16)
+                cols = slice(u[0], u[0] + u[1])
+                put(self.k_half[u, hh], there.at[hh, :, :, cols], back.at[hh, :, :, cols], sib)
+
+        def second_own(self, u):
             for hh in range(2):
-
-                def tile(n, _, hh=hh):
-                    cols = pl.ds(pl.multiple_of(n * 256, 256), 256)
-                    kept = jnp.dot(self.hid[...], wout[2 * hh + c, :, cols], preferred_element_type=F32)
-                    self.part[hh, :, :, cols] = kept.reshape(4, self.n, 256)
-                    return 0
-
-                lax.fori_loop(0, 3, tile, 0)
-
-        def halves(self):
+                for at, cols, value in self.second(c, hh, u):
+                    self.part[hh, :, :, at : at + cols] = value.reshape(4, self.n, cols)
+
+        def halves(self, u):
             back = obr[self.p].at[self.it]
+            cols = slice(u[0], u[0] + u[1])
             for hh in range(2):
-                got(self.k_half[hh], back.at[hh])
-                self.part[hh] += back[hh].astype(F32).reshape(4, self.n, 2 * W)
-
-        def term(self, d, j):
-            return self.part[d // 4, lax.rem(d, 4), :, W * j : W * (j + 1)]
-
-        def scatter(self, s):
+                got(self.k_half[u, hh], back.at[hh, :, :, cols])
+                for j in range(2):
+                    at = slice(W * j + u[0], W * j + u[0] + u[1])
+                    self.part[hh, :, :, at] += back[hh, j, :, cols].astype(F32).reshape(4, self.n, u[1])
+
+        def term(self, d, j, u):
+            return self.part[d // 4, lax.rem(d, 4), :, W * j + u[0] : W * j + u[0] + u[1]]
+
+        def scatter(self, s, u):
+            k = self.k_sum[u]
+            cols = slice(u[0], u[0] + u[1])
             out, back = rss[self.p].at[self.it], rsr[self.p].at[self.it]
             for j in range(2):
                 for g in range(2):
-                    if (s, g, j) not in self.k_sum:
+                    if (s, g, j) not in k:
                         continue
-                    value = self.term(zo(sign[g] * (5 - s)), j)
-                    if (s - 1, g, j) in self.k_sum:
-                        got(self.k_sum[s - 1, g, j], back.at[s - 2, g, j])
-                        value = value + back[s - 2, g, j].astype(F32)
-                    out[s - 1, g, j] = value.astype(BF16)
-                    put(self.k_sum[s, g, j], out.at[s - 1, g, j], back.at[s - 1, g, j], dev(z_=zo(sign[g])))
-
-        def scattered(self):
+                    value = self.term(zo(sign[g] * (5 - s)), j, u)
+                    if (s - 1, g, j) in k:
+                        got(k[s - 1, g, j], back.at[s - 2, g, j, :, cols])
+                        value = value + back[s - 2, g, j, :, cols].astype(F32)
+                    out[s - 1, g, j, :, cols] = value.astype(BF16)
+                    here, there = out.at[s - 1, g, j, :, cols], back.at[s - 1, g, j, :, cols]
+                    put(k[s, g, j], here, there, dev(z_=zo(sign[g])))
+
+        def scattered(self, u):
+            k = self.k_sum[u]
+            cols = slice(u[0], u[0] + u[1])
             back = rsr[self.p].at[self.it]
-            self.drift = []
             for j in range(2):
-                value = self.term(z, j)
+                value = self.term(z, j, u)
                 for g in range(2):
-                    got(self.k_sum[4, g, j], back.at[3, g, j])
-                    value = value + back[3, g, j].astype(F32)
-                self.drift.append(step_ref[0] * mod(j, 2) * value)
+                    got(k[4, g, j], back.at[3, g, j, :, cols])
+                    value = value + back[3, g, j, :, cols].astype(F32)
+                drift[self.p][j, :, cols] = step_ref[0] * mod(j, 2)[:, cols] * value
 
         def prefix_copy(self, i):
             return remote(
@@ -375,7 +372,7 @@
 
         def prefix_send(self):
             for j in range(2):
-                dsend[self.p][j] = self.drift[j].astype(BF16)
+                dsend[self.p][j] = drift[self.p][j].astype(BF16)
             for i in (1, 2, 3):
 
                 @pl.when(y + i < 4)
@@ -410,7 +407,7 @@
         def out_send(self):
             self.k_out = {(k, i): next(ids) for k in range(4) for i in range(2)}
             for i in range(2):
-                fsend[self.p][i] = self.drift[i].astype(BF16)
+                fsend[self.p][i] = drift[self.p][i].astype(BF16)
             for k in (3, 2, 1, 0):
                 for i in range(2):
                     if k:
@@ -457,12 +454,15 @@
     swap_in(ks_state, sbuf)
     for v in (a, b):
         v.stats([sbuf[j, v.rows(), :] for j in range(2)])
+    w_in.arrive(4)
     got(k_ms, mrecv.at[0])
     m1[...] = mbuf[...] + mrecv[0]
     k_ml = {k: next(ids) for k in (1, 2, 3)}
     for k in (1, 2, 3):
         put(k_ml[k], m1, mrecv.at[k], lo(k))
-    weight_far(0)
+    w_in.arrive(0)
+    w_a.near_start()
+    w_b.cross_start()
     for k in (1, 2, 3):
         got(k_ml[k], mrecv.at[k])
     m2[...] = m1[...] + mrecv[1] + mrecv[2] + mrecv[3]
@@ -470,90 +470,122 @@
     for k in (1, 2, 3):
         put(k_mx[k], m2, modall.at[x], dev(x_=xo(k)))
     modall[x] = m2[...]
-    weight_far(1)
-    near_start(1)
+    w_a.arrive(4)
+    w_in.spread(4)
     for k in (1, 2, 3):
         got(k_mx[k], modall.at[xo(-k)])
     for v in (a, b):
         v.normalise()
-    weight_near(0)
-    weight_far_y(0, 0)
+    w_in.arrive(1)
+    w_in.arrive(3)
+    w_in.spread(0)
     for v in (a, b):
         v.gather(1)
-    weight_far_x(0, 1)
-    weight_far_x(0, 3)
-    weight_far_y(1, 0)
+    w_in.arrive(2)
+    w_a.arrive(0)
+    w_b.near_start()
+    w_a.spread(4)
     for v in (a, b):
         v.gather(2)
-    weight_far_x(0, 2)
-    weight_far_x(1, 1)
-    weight_far_x(1, 3)
-    weight_far_y(0, 1)
+    w_in.spread(1)
+    w_in.spread(3)
+    w_a.arrive(1)
+    w_a.arrive(3)
     for v in (a, b):
         v.gather(3)
-    weight_far_y(0, 3)
-    weight_far_x(1, 2)
-    weight_far_y(0, 2)
+    w_in.spread(2)
+    w_a.arrive(2)
+    w_a.spread(0)
+    w_b.arrive(4)
+    w_b.arrive(0)
     for v in (a, b):
         v.gather(4)
-    weight_near(1)
-    weight_far_y(1, 1)
-    weight_far_y(1, 3)
-    swap_in(ks_anchor, abuf)
+    w_a.spread(1)
+    w_a.spread(3)
+    w_b.arrive(1)
+    w_b.arrive(3)
+    w_b.arrive(2)
+    w_a.spread(2)
+    w_b.spread(4)
     a.gathered()
     b.gathered()
-    weight_far_y(1, 2)
-    weight_end(0)
+    w_in.end()
     a.first_matmul()
+    w_b.spread(0)
     b.first_matmul()
-    weight_end(1)
-    for it in range(ITERS):
-        a, b = parts[it]
-        if it:
-            a.gathered()
-            a.first_matmul()
-        a.second_other()
-        a.second_own()
-        if it:
-            b.gather(4)
-            b.gathered()
-        a.halves()
-        a.scatter(1)
-        if it:
-            b.first_matmul()
-        b.second_other()
-        a.scatter(2)
-        b.second_own()
-        b.halves()
-        b.scatter(1)
-        a.scatter(3)
-        b.scatter(2)
-        a.scatter(4)
-        b.scatter(3)
-        a.scattered()
-        if it + 1 == ITERS:
-            a.out_send()
-            b.scatter(4)
-            b.scattered()
-            b.out_send()
-            a.out_add()
-            b.out_add()
-            continue
-        a.prefix_send()
-        b.scatter(4)
-        b.scattered()
-        b.prefix_send()
-        c1, d1 = parts[it + 1]
-        a.prefix_add()
-        c1.stats(a.current())
-        b.prefix_add()
-        d1.stats(b.current())
-        c1.normalise()
-        d1.normalise()
-        for s in range(1, 4):
-            c1.gather(s)
-            d1.gather(s)
-        c1.gather(4)
+    w_b.spread(1)
+    w_b.spread(3)
+    ua, ub = UNITS
+    w_a.end()
+    for v in (a, b):
+        v.second_other(ua)
+    w_b.spread(2)
+    for v in (a, b):
+        v.second_own(ua)
+    ks_anchor = swap_out(lambda i: a_ref.at[pl.ds(T * i, T)], abuf)
+    for v in (a, b):
+        v.halves(ua)
+        v.scatter(1, ua)
+    for v in (a, b):
+        v.scatter(2, ua)
+    w_b.end()
+    a.second_other(ub)
+    a.scatter(3, ua)
+    a.second_own(ub)
+    b.scatter(3, ua)
+    b.second_other(ub)
+    a.scatter(4, ua)
+    b.second_own(ub)
+    b.scatter(4, ua)
+    for v in (a, b):
+        v.halves(ub)
+        v.scatter(1, ub)
+    for s in (2, 3, 4):
+        for v in (a, b):
+            v.scatter(s, ub)
+            if s == 2:
+                v.scattered(ua)
+    swap_in(ks_anchor, abuf)
+    for v in (a, b):
+        v.scattered(ub)
+        v.prefix_send()
+    e, f = parts[1]
+    a.prefix_add()
+    e.stats(a.current())
+    b.prefix_add()
+    f.stats(b.current())
+    e.normalise()
+    f.normalise()
+    for s in range(1, 4):
+        e.gather(s)
+        f.gather(s)
+    e.gather(4)
+    e.gathered()
+    u = (0, W)
+    e.first_matmul()
+    e.second_other(u)
+    e.second_own(u)
+    f.gather(4)
+    f.gathered()
+    e.halves(u)
+    e.scatter(1, u)
+    f.first_matmul()
+    f.second_other(u)
+    e.scatter(2, u)
+    f.second_own(u)
+    f.halves(u)
+    f.scatter(1, u)
+    e.scatter(3, u)
+    f.scatter(2, u)
+    e.scatter(4, u)
+    f.scatter(3, u)
+    e.scattered(u)
+    e.out_send()
+    f.scatter(4, u)
+    f.scattered(u)
+    f.out_send()
+    e.out_add()
+    f.out_add()
 
     for copy in pending:
         copy.wait_send()
@@ -599,14 +631,15 @@
         each(lambda n: pltpu.VMEM((ITERS, 3, n, 128), F32)),
         each(lambda n: pltpu.VMEM((ITERS, 4 * n, D), BF16)),
         each(lambda n: pltpu.VMEM((4 * n, U), BF16)),
-        each(lambda n: pltpu.VMEM((ITERS, 2, 4 * n, 2 * W), BF16)),
-        each(lambda n: pltpu.VMEM((ITERS, 2, 4 * n, 2 * W), BF16)),
+        each(lambda n: pltpu.VMEM((ITERS, 2, 2, 4 * n, W), BF16)),
+        each(lambda n: pltpu.VMEM((ITERS, 2, 2, 4 * n, W), BF16)),
         each(lambda n: pltpu.VMEM((2, 4, n, 2 * W), F32)),
         each(lambda n: pltpu.VMEM((ITERS, 4, 2, 2, n, W), BF16)),
         each(lambda n: pltpu.VMEM((ITERS, 4, 2, 2, n, W), BF16)),
         each(lambda n: pltpu.VMEM((2, n, W), BF16)),
         each(lambda n: pltpu.VMEM((3, 2, n, W), BF16)),
         each(lambda n: pltpu.VMEM((2, n, W), BF16)),
+        each(lambda n: pltpu.VMEM((2, n, W), F32)),
         pltpu.SemaphoreType.DMA((COPIES,)),
         pltpu.SemaphoreType.DMA((COPIES,)),
     ]

time: 161 us -> 179 us (1.11)
  Pallas kernels: 156 us -> 175 us
    pallas_call x1, Pallas kernels: 156 us -> 175 us  [local(): pl.pallas_call(kernel, out_shape=jax.ShapeDtypeStruct(anchor.shape, F32),...]
where the time goes in v3:
time: 179 us
  Pallas kernels  175 us (98%)
  local copies, waits for them, and re-layouts  2.27 us (1%)
    pallas_call x1, Pallas kernels, local(): pl.pallas_call(kernel, out_shape=jax.ShapeDtypeStruct(anchor.shape, F32),...  175 us

profile of v3, /device:TPU:17, one launch (start us, length us, event | category | flops | bytes accessed | tf_op | source)
XLA Modules:
  0.0 178.9 jit_solution(18149756086049807980)
XLA Ops:
  0.0 0.0 copy-start
  1.4 0.2 fusion
  1.6 0.0 copy-done
  1.6 0.5 fusion.3
  2.1 0.6 copy.10
  2.7 174.5 %picard.1 = f32[160,384]{1,0:T(8,128)} custom-call(f32[1]{0:T(128)S(6)} %copy.13.step_ref, f32[160,384]{1,0:T(8,128)} %bitcast.11, f32[160,384]{1,0:T(8,128)} %a_ref.1, f32[3,384]{1,0:T(4,128)} %bitcast.12, bf16[384,1536]{1,0:T(8,128)(2,1)} %wi_ref.1, bf16[1536,384]{1,0:T(8,128)(2,1)} %wo_ref.1), custom_call_target="tpu_custom_call" | custom-call | tf_op jit(solution)/shard_map/picard/pallas_call | solution.py:646
  177.2 1.7 copy.14
Async XLA Ops:
  0.0 1.6 copy-start

commit v4 on v3

--- a/solution.py
+++ b/solution.py
@@ -20,8 +20,7 @@
 
 PARTS = ((0, 48), (48, 32))
 
-UNITS = ((0, 256), (256, 128))
-COPIES = 400
+COPIES = 304
 
 
 def timestep_embedding(timesteps):
@@ -34,7 +33,7 @@
 
 def kernel(
     step_ref, s_ref, a_ref, m_ref, wi_ref, wo_ref, out_ref,
-    sbuf, abuf, mbuf, m1, m2, mrecv, modall, win, wout, pref, frecv,
+    sbuf, abuf, modx, msib, m1, mrecv, modall, win, wout, pref, frecv,
     stat, statr, xall, hid, obs, obr, part, rss, rsr, dsend, drecv, fsend, drift,
     send, recv,
 ):
@@ -128,12 +127,12 @@
         for i in range(2):
             got(ks[i], dst.at[i])
 
+    k_mx = {k: next(ids) for k in (1, 2, 3)}
+    modx[x] = jnp.zeros((8, W), F32)
+    modx[x, 0:3, :] = m_ref[...]
+    for k in (1, 2, 3):
+        put(k_mx[k], modx.at[x], modx.at[x], dev(x_=xo(k)))
     ks_state = swap_out(lambda i: s_ref.at[pl.ds(T * i, T)], sbuf)
-
-    mbuf[...] = jnp.zeros_like(mbuf)
-    mbuf[0:3, :] = m_ref[...]
-    k_ms = next(ids)
-    put(k_ms, mbuf, mrecv.at[0], sib)
 
     mine = 4 * h + x
     far = 4 * (1 - h)
@@ -161,11 +160,13 @@
         return part_of, slot_of, U
 
     class Side:
-        def __init__(self, part_of, slot_of, rows):
+        def __init__(self, part_of, slot_of, rows, cross):
             self.part_of, self.slot_of, self.rows, self.q = part_of, slot_of, rows, rows // 4
+            self.flows = range(5 if cross else 4)
             self.k_x = {k: next(ids) for k in (1, 3)}
-            self.k_in = [next(ids) for _ in range(5)]
-            self.k_y = {(s, k, f): next(ids) for s in range(5) for k in (1, 3) for f in range(2)}
+            self.k_fwd = {} if cross else {k: next(ids) for k in (1, 3)}
+            self.k_in = [next(ids) for _ in self.flows]
+            self.k_y = {(s, k, f): next(ids) for s in self.flows for k in (1, 3) for f in range(2)}
             self.k_own = next(ids)
 
         def quarter(self, s, yy, first=0, rows=None):
@@ -200,25 +201,31 @@
                 there = self.quarter(s, yo(-k), first, self.q // 2)
                 put(self.k_y[s, k, 1], there, there, dev(y_=yo(k)))
 
+        def forward(self):
+            for k, first in ((1, 0), (3, self.rows // 2)):
+                got(self.k_x[k], self.slot_of(4 * h + xo(-k)))
+                there = self.slot_of(4 * h + xo(-k), first, self.rows // 2)
+                put(self.k_fwd[k], there, there, dev(x_=xo(k)))
+
         def end(self):
-            for k in (1, 3):
-                got(self.k_x[k], self.slot_of(4 * h + xo(-k)))
-            for s in range(5):
+            for k, first in ((1, 0), (3, self.rows // 2)):
+                if self.k_fwd:
+                    got(self.k_fwd[k], self.slot_of(4 * h + xo(2), first, self.rows // 2))
+                else:
+                    got(self.k_x[k], self.slot_of(4 * h + xo(-k)))
+            for s in self.flows:
                 for k, first in ((1, 0), (3, self.q // 2)):
                     got(self.k_y[s, k, 1], self.quarter(s, yo(2), first, self.q // 2))
             self.copy.wait()
 
-    w_in = Side(*win_side())
-    w_a, w_b = (Side(*wout_side(*unit)) for unit in UNITS)
+    w_in = Side(*win_side(), True)
+    w_out = Side(*wout_side(0, W), False)
     w_in.cross_start()
     w_in.far_start()
     w_in.near_start()
-    w_a.far_start()
-    w_a.cross_start()
-    w_b.far_start()
 
     def mod(j, r):
-        return modall[2 * c + j, r : r + 1, :]
+        return modall[j, r : r + 1, :]
 
     sign = (1, -1)
 
@@ -232,7 +239,7 @@
             self.k_ring = {key: next(ids) for key in steps if key[0] < 4 or key[1] == key[2]}
             self.k_sib = {key: next(ids) for key in self.k_ring}
             self.k_own = [next(ids) for _ in range(2)]
-            self.units = ((0, W),) if it else UNITS
+            self.units = ((0, W),)
             self.k_half = {(u, hh): next(ids) for u in self.units for hh in range(2)}
             self.k_sum = {
                 u: {key: next(ids) for key in steps if key[0] > 1 or key[1] == key[2]} for u in self.units
@@ -451,141 +458,109 @@
     parts = [[Part(it, p) for p in range(2)] for it in range(ITERS)]
     a, b = parts[0]
 
+    for k in (1, 2, 3):
+        got(k_mx[k], modx.at[xo(-k)])
+    k_ms = next(ids)
+    put(k_ms, modx.at[pl.ds(2 * (1 - c), 2)], msib, sib)
     swap_in(ks_state, sbuf)
     for v in (a, b):
         v.stats([sbuf[j, v.rows(), :] for j in range(2)])
-    w_in.arrive(4)
-    got(k_ms, mrecv.at[0])
-    m1[...] = mbuf[...] + mrecv[0]
+    w_out.far_start()
+    got(k_ms, msib)
+    m1[...] = modx[pl.ds(2 * c, 2)] + msib[...]
     k_ml = {k: next(ids) for k in (1, 2, 3)}
     for k in (1, 2, 3):
-        put(k_ml[k], m1, mrecv.at[k], lo(k))
+        put(k_ml[k], m1, mrecv.at[k - 1], lo(k))
+    w_in.arrive(4)
     w_in.arrive(0)
-    w_a.near_start()
-    w_b.cross_start()
+    w_in.spread(4)
+    w_out.arrive(0)
+    w_out.near_start()
+    w_in.spread(0)
     for k in (1, 2, 3):
-        got(k_ml[k], mrecv.at[k])
-    m2[...] = m1[...] + mrecv[1] + mrecv[2] + mrecv[3]
-    k_mx = {k: next(ids) for k in (1, 2, 3)}
-    for k in (1, 2, 3):
-        put(k_mx[k], m2, modall.at[x], dev(x_=xo(k)))
-    modall[x] = m2[...]
-    w_a.arrive(4)
-    w_in.spread(4)
-    for k in (1, 2, 3):
-        got(k_mx[k], modall.at[xo(-k)])
+        got(k_ml[k], mrecv.at[k - 1])
+    modall[...] = m1[...] + mrecv[0] + mrecv[1] + mrecv[2]
     for v in (a, b):
         v.normalise()
+    w_out.spread(0)
+    w_in.arrive(2)
+    for v in (a, b):
+        v.gather(1)
     w_in.arrive(1)
     w_in.arrive(3)
-    w_in.spread(0)
-    for v in (a, b):
-        v.gather(1)
-    w_in.arrive(2)
-    w_a.arrive(0)
-    w_b.near_start()
-    w_a.spread(4)
     for v in (a, b):
         v.gather(2)
+    w_in.spread(2)
+    w_out.arrive(2)
     w_in.spread(1)
-    w_in.spread(3)
-    w_a.arrive(1)
-    w_a.arrive(3)
+    w_out.arrive(1)
+    w_out.arrive(3)
     for v in (a, b):
         v.gather(3)
-    w_in.spread(2)
-    w_a.arrive(2)
-    w_a.spread(0)
-    w_b.arrive(4)
-    w_b.arrive(0)
+    w_in.spread(3)
     for v in (a, b):
         v.gather(4)
-    w_a.spread(1)
-    w_a.spread(3)
-    w_b.arrive(1)
-    w_b.arrive(3)
-    w_b.arrive(2)
-    w_a.spread(2)
-    w_b.spread(4)
+    w_out.spread(2)
+    w_out.spread(1)
+    w_out.forward()
+    w_out.spread(3)
     a.gathered()
     b.gathered()
     w_in.end()
     a.first_matmul()
-    w_b.spread(0)
     b.first_matmul()
-    w_b.spread(1)
-    w_b.spread(3)
-    ua, ub = UNITS
-    w_a.end()
-    for v in (a, b):
-        v.second_other(ua)
-    w_b.spread(2)
-    for v in (a, b):
-        v.second_own(ua)
+    w_out.end()
     ks_anchor = swap_out(lambda i: a_ref.at[pl.ds(T * i, T)], abuf)
-    for v in (a, b):
-        v.halves(ua)
-        v.scatter(1, ua)
-    for v in (a, b):
-        v.scatter(2, ua)
-    w_b.end()
-    a.second_other(ub)
-    a.scatter(3, ua)
-    a.second_own(ub)
-    b.scatter(3, ua)
-    b.second_other(ub)
-    a.scatter(4, ua)
-    b.second_own(ub)
-    b.scatter(4, ua)
-    for v in (a, b):
-        v.halves(ub)
-        v.scatter(1, ub)
-    for s in (2, 3, 4):
-        for v in (a, b):
-            v.scatter(s, ub)
-            if s == 2:
-                v.scattered(ua)
-    swap_in(ks_anchor, abuf)
-    for v in (a, b):
-        v.scattered(ub)
-        v.prefix_send()
-    e, f = parts[1]
-    a.prefix_add()
-    e.stats(a.current())
-    b.prefix_add()
-    f.stats(b.current())
-    e.normalise()
-    f.normalise()
-    for s in range(1, 4):
-        e.gather(s)
-        f.gather(s)
-    e.gather(4)
-    e.gathered()
+
     u = (0, W)
-    e.first_matmul()
-    e.second_other(u)
-    e.second_own(u)
-    f.gather(4)
-    f.gathered()
-    e.halves(u)
-    e.scatter(1, u)
-    f.first_matmul()
-    f.second_other(u)
-    e.scatter(2, u)
-    f.second_own(u)
-    f.halves(u)
-    f.scatter(1, u)
-    e.scatter(3, u)
-    f.scatter(2, u)
-    e.scatter(4, u)
-    f.scatter(3, u)
-    e.scattered(u)
-    e.out_send()
-    f.scatter(4, u)
-    f.scattered(u)
-    f.out_send()
-    e.out_add()
-    f.out_add()
+    for it in range(ITERS):
+        a, b = parts[it]
+        if it:
+            a.gathered()
+            a.first_matmul()
+        a.second_other(u)
+        a.second_own(u)
+        if it:
+            b.gather(4)
+            b.gathered()
+        a.halves(u)
+        a.scatter(1, u)
+        if it:
+            b.first_matmul()
+        b.second_other(u)
+        a.scatter(2, u)
+        b.second_own(u)
+        b.halves(u)
+        b.scatter(1, u)
+        a.scatter(3, u)
+        b.scatter(2, u)
+        a.scatter(4, u)
+        b.scatter(3, u)
+        a.scattered(u)
+        if it + 1 == ITERS:
+            a.out_send()
+            b.scatter(4, u)
+            b.scattered(u)
+            b.out_send()
+            a.out_add()
+            b.out_add()
+            continue
+        a.prefix_send()
+        b.scatter(4, u)
+        b.scattered(u)
+        b.prefix_send()
+        swap_in(ks_anchor, abuf)
+        after, later = parts[it + 1]
+        a.prefix_add()
+        after.stats(a.current())
+        b.prefix_add()
+        later.stats(b.current())
+        after.normalise()
+        later.normalise()
+        for s in range(1, 4):
+            after.gather(s)
+            later.gather(s)
+        after.gather(4)
 
     for copy in pending:
         copy.wait_send()
@@ -618,11 +593,11 @@
     scratch = [
         pltpu.VMEM((2, T, W), F32),
         pltpu.VMEM((2, T, W), F32),
-        pltpu.VMEM((8, W), F32),
-        pltpu.VMEM((8, W), F32),
-        pltpu.VMEM((8, W), F32),
         pltpu.VMEM((4, 8, W), F32),
-        pltpu.VMEM((4, 8, W), F32),
+        pltpu.VMEM((2, 8, W), F32),
+        pltpu.VMEM((2, 8, W), F32),
+        pltpu.VMEM((3, 2, 8, W), F32),
+        pltpu.VMEM((2, 8, W), F32),
         pltpu.VMEM((D, U), BF16),
         pltpu.VMEM((4, U, 2 * W), BF16),
         pltpu.VMEM((2, T, W), F32),

time: 179 us -> 152 us (0.85)
  Pallas kernels: 175 us -> 147 us
    pallas_call x1, Pallas kernels: 175 us -> 147 us  [local(): pl.pallas_call(kernel, out_shape=jax.ShapeDtypeStruct(anchor.shape, F32),...]
where the time goes in v4:
time: 152 us
  Pallas kernels  147 us (97%)
  local copies, waits for them, and re-layouts  2.27 us (1%)
    pallas_call x1, Pallas kernels, local(): pl.pallas_call(kernel, out_shape=jax.ShapeDtypeStruct(anchor.shape, F32),...  147 us

profile of v4, /device:TPU:17, one launch (start us, length us, event | category | flops | bytes accessed | tf_op | source)
XLA Modules:
  0.0 151.6 jit_solution(11633897742315485288)
XLA Ops:
  0.0 0.0 copy-start
  1.4 0.2 fusion
  1.6 0.0 copy-done
  1.6 0.5 fusion.3
  2.1 0.6 copy.10
  2.7 147.3 %picard.1 = f32[160,384]{1,0:T(8,128)} custom-call(f32[1]{0:T(128)S(6)} %copy.13.step_ref, f32[160,384]{1,0:T(8,128)} %bitcast.11, f32[160,384]{1,0:T(8,128)} %a_ref.1, f32[3,384]{1,0:T(4,128)} %bitcast.12, bf16[384,1536]{1,0:T(8,128)(2,1)} %wi_ref.1, bf16[1536,384]{1,0:T(8,128)(2,1)} %wo_ref.1), custom_call_target="tpu_custom_call" | custom-call | tf_op jit(solution)/shard_map/picard/pallas_call | solution.py:621
  150.0 1.7 %copy.14 = f32[1,160,384]{2,1,0:T(8,128)} copy(f32[1,160,384]{2,1,0:T(8,128)} %bitcast.10) | data formatting | bytes 491520
Async XLA Ops:
  0.0 1.6 %copy-start = (bf16[384,3,384]{2,0,1:T(8,128)(2,1)S(1)}, bf16[384,3,384]{2,0,1:T(8,128)(2,1)}, u32[]{:S(2)}) copy-start(bf16[384,3,384]{2,0,1:T(8,128)(2,1)} %param.13) | copy-start | bytes 2654212

commit v5 on v4

--- a/solution.py
+++ b/solution.py
@@ -18,21 +18,16 @@
 W = 384
 U = 768
 
-PARTS = ((0, 48), (48, 32))
+PARTS = ((0, 32), (32, 48))
+
+ORDER = ((0, 0), (1, 1), (0, 1), (1, 0))
 
 COPIES = 304
 
 
-def timestep_embedding(timesteps):
-    half_width = D // 2
-    positions = jnp.arange(half_width, dtype=jnp.float32)
-    frequency = jnp.exp(-math.log(10000.0) * positions / half_width)
-    phases = timesteps.astype(jnp.float32)[:, None] * frequency[None, :]
-    return jnp.concatenate([jnp.cos(phases), jnp.sin(phases)], axis=1)
-
-
 def kernel(
-    step_ref, s_ref, a_ref, m_ref, wi_ref, wo_ref, out_ref,
+    time_any, step_any, s_ref, a_any, m_any, wi_ref, wo_ref, out_ref,
+    time_ref, step_ref, a_ref, m_ref,
     sbuf, abuf, modx, msib, m1, mrecv, modall, win, wout, pref, frecv,
     stat, statr, xall, hid, obs, obr, part, rss, rsr, dsend, drecv, fsend, drift,
     send, recv,
@@ -83,6 +78,11 @@
 
     def got(k, dst):
         remote(dst, dst, k, k, sib).wait_recv()
+
+    loads = [(time_any, time_ref), (m_any, m_ref), (step_any, step_ref)]
+    loads = [pltpu.make_async_copy(*pair, recv.at[next(ids)]) for pair in loads]
+    for copy in loads:
+        copy.start()
 
     partners = [sib, z4, z4sib, dev(z_=zo(1)), dev(z_=zo(-1))]
     partners += [dev(x_=xo(k)) for k in (1, 2, 3)]
@@ -104,6 +104,21 @@
         def _(i=i):
             pl.semaphore_signal(barrier, inc=1, device_id=swap[i], device_id_type=MESH)
 
+    for copy in loads[:2]:
+        copy.wait()
+
+    entry = (lax.rem(row, 4) * W + lax.broadcasted_iota(jnp.int32, (16, W), 1)).astype(F32)
+    phase = time_ref[0].astype(F32) * jnp.exp(-math.log(10000.0) * entry / (D // 2))
+    embedding = jnp.where(row < 4, jnp.cos(phase), jnp.sin(phase))
+    high = embedding.astype(BF16).astype(F32)
+    middle = (embedding - high).astype(BF16).astype(F32)
+    low = embedding - high - middle
+    line = lax.broadcasted_iota(jnp.int32, (16, W), 0)
+    terms = jnp.where(line == 0, high, jnp.where(line == 1, middle, jnp.where(line == 2, low, 0.0)))
+    modx[x] = jnp.zeros((8, W), F32)
+    for r in range(3):
+        products = jnp.dot(terms.astype(BF16), m_ref[r], preferred_element_type=F32)
+        modx[x, r : r + 1, :] = jnp.sum(products, axis=0, keepdims=True)
     pl.semaphore_wait(barrier, len(partners) + len(swap_y) + 2 - same.astype(jnp.int32))
 
     swaps = []
@@ -128,8 +143,6 @@
             got(ks[i], dst.at[i])
 
     k_mx = {k: next(ids) for k in (1, 2, 3)}
-    modx[x] = jnp.zeros((8, W), F32)
-    modx[x, 0:3, :] = m_ref[...]
     for k in (1, 2, 3):
         put(k_mx[k], modx.at[x], modx.at[x], dev(x_=xo(k)))
     ks_state = swap_out(lambda i: s_ref.at[pl.ds(T * i, T)], sbuf)
@@ -278,20 +291,22 @@
                 value = (self.cur[j] - mean) * scale * (1.0 + mod(j, 1)) + mod(j, 0)
                 slot = self.slot(z, c, j)
                 slot[...] = value.astype(BF16)
-                for g in range(2):
-                    put(self.k_ring[1, g, j], slot, slot, dev(z_=zo(sign[g])))
+            for g, j in ORDER:
+                slot = self.slot(z, c, j)
+                put(self.k_ring[1, g, j], slot, slot, dev(z_=zo(sign[g])))
+            for j in range(2):
+                slot = self.slot(z, c, j)
                 put(self.k_own[j], slot, slot, sib)
 
         def gather(self, s):
-            for j in range(2):
-                for g in range(2):
-                    if (s, g, j) not in self.k_ring:
-                        continue
-                    slot = self.slot(zo(-sign[g] * s), c, j)
-                    got(self.k_ring[s, g, j], slot)
-                    if (s + 1, g, j) in self.k_ring:
-                        put(self.k_ring[s + 1, g, j], slot, slot, dev(z_=zo(sign[g])))
-                    put(self.k_sib[s, g, j], slot, slot, sib)
+            for g, j in ORDER:
+                if (s, g, j) not in self.k_ring:
+                    continue
+                slot = self.slot(zo(-sign[g] * s), c, j)
+                got(self.k_ring[s, g, j], slot)
+                if (s + 1, g, j) in self.k_ring:
+                    put(self.k_ring[s + 1, g, j], slot, slot, dev(z_=zo(sign[g])))
+                put(self.k_sib[s, g, j], slot, slot, sib)
 
         def gathered(self):
             for j in range(2):
@@ -349,17 +364,17 @@
             k = self.k_sum[u]
             cols = slice(u[0], u[0] + u[1])
             out, back = rss[self.p].at[self.it], rsr[self.p].at[self.it]
-            for j in range(2):
-                for g in range(2):
-                    if (s, g, j) not in k:
-                        continue
-                    value = self.term(zo(sign[g] * (5 - s)), j, u)
-                    if (s - 1, g, j) in k:
-                        got(k[s - 1, g, j], back.at[s - 2, g, j, :, cols])
-                        value = value + back[s - 2, g, j, :, cols].astype(F32)
-                    out[s - 1, g, j, :, cols] = value.astype(BF16)
-                    here, there = out.at[s - 1, g, j, :, cols], back.at[s - 1, g, j, :, cols]
-                    put(k[s, g, j], here, there, dev(z_=zo(sign[g])))
+            for g, j in ORDER:
+                t = s if g == j else s + 1
+                if t > 4:
+                    continue
+                value = self.term(zo(sign[g] * (5 - t)), j, u)
+                if (t - 1, g, j) in k:
+                    got(k[t - 1, g, j], back.at[t - 2, g, j, :, cols])
+                    value = value + back[t - 2, g, j, :, cols].astype(F32)
+                out[t - 1, g, j, :, cols] = value.astype(BF16)
+                here, there = out.at[t - 1, g, j, :, cols], back.at[t - 1, g, j, :, cols]
+                put(k[t, g, j], here, there, dev(z_=zo(sign[g])))
 
         def scattered(self, u):
             k = self.k_sum[u]
@@ -447,7 +462,7 @@
         def out_add(self):
             for i in range(2):
                 rows = slice(T * i + self.first, T * i + self.first + self.n)
-                out_ref[rows, :] = a_ref[rows, :]
+                out_ref[rows, :] = jnp.zeros((self.n, W), F32)
                 for k in (3, 2, 1, 0):
 
                     @pl.when(y - k >= 0)
@@ -457,6 +472,9 @@
 
     parts = [[Part(it, p) for p in range(2)] for it in range(ITERS)]
     a, b = parts[0]
+
+    for copy in loads[2:]:
+        copy.wait()
 
     for k in (1, 2, 3):
         got(k_mx[k], modx.at[xo(-k)])
@@ -510,7 +528,7 @@
     a.first_matmul()
     b.first_matmul()
     w_out.end()
-    ks_anchor = swap_out(lambda i: a_ref.at[pl.ds(T * i, T)], abuf)
+    ks_anchor = swap_out(lambda i: a_any.at[pl.ds(T * i, T)], abuf)
 
     u = (0, W)
     for it in range(ITERS):
@@ -528,8 +546,8 @@
         if it:
             b.first_matmul()
         b.second_other(u)
+        b.second_own(u)
         a.scatter(2, u)
-        b.second_own(u)
         b.halves(u)
         b.scatter(1, u)
         a.scatter(3, u)
@@ -577,20 +595,16 @@
 
 
 def local(states, anchor, timesteps, step_sizes, weight_in, weight_out, mod_weight):
-    embedding = timestep_embedding(timesteps)[0]
-    rows_here = mod_weight.shape[0]
-    embed_part = lax.dynamic_slice_in_dim(
-        embedding, lax.axis_index("row") * rows_here, rows_here, 0
-    )
-    mod_part = jnp.einsum(
-        "e,ekd->kd", embed_part, mod_weight.astype(jnp.float32), precision=lax.Precision.HIGHEST
-    )
     vmem = pl.BlockSpec(memory_space=pltpu.VMEM)
 
     def each(make):
         return [make(n) for _, n in PARTS]
 
     scratch = [
+        pltpu.SMEM((1,), jnp.int32),
+        pltpu.SMEM((1,), F32),
+        pltpu.VMEM(anchor.shape, F32),
+        pltpu.VMEM((3, W, W), BF16),
         pltpu.VMEM((2, T, W), F32),
         pltpu.VMEM((2, T, W), F32),
         pltpu.VMEM((4, 8, W), F32),
@@ -621,16 +635,15 @@
     out = pl.pallas_call(
         kernel,
         out_shape=jax.ShapeDtypeStruct(anchor.shape, F32),
-        in_specs=[pl.BlockSpec(memory_space=pltpu.SMEM), vmem, vmem, vmem]
-        + [pl.BlockSpec(memory_space=pl.ANY)] * 2,
+        in_specs=[pl.BlockSpec(memory_space=pl.ANY)] * 7,
         out_specs=vmem,
         scratch_shapes=scratch,
         compiler_params=pltpu.CompilerParams(
             collective_id=0, has_side_effects=True, vmem_limit_bytes=60 << 20
         ),
         name="picard",
-    )(step_sizes, states[0], anchor, mod_part, weight_in, weight_out)
-    return out[None]
+    )(timesteps, step_sizes, states[0], anchor, mod_weight.transpose(1, 0, 2), weight_in, weight_out)
+    return (anchor + out)[None]
 
 
 def solution(mesh):

time: 152 us -> 145 us (0.954)
  Pallas kernels: 147 us -> 142 us
  local copies, waits for them, and re-layouts: 2.27 us -> 0.01 us
    pallas_call x1, Pallas kernels: 147 us -> 142 us  [local(): pl.pallas_call(kernel, out_shape=jax.ShapeDtypeStruct(anchor.shape, F32),...]
    broadcast_in_dim x0 -> x1, other arithmetic: none -> 1.66 us  [local(): return (anchor + out)[None]]
    unnamed x3 -> x2, local copies, waits for them, and re-layouts: 1.66 us -> 0.01 us
where the time goes in v5:
time: 145 us
  Pallas kernels  142 us (98%)
  other arithmetic  1.66 us (1%)
    pallas_call x1, Pallas kernels, local(): pl.pallas_call(kernel, out_shape=jax.ShapeDtypeStruct(anchor.shape, F32),...  142 us

profile of v5, /device:TPU:17, one launch (start us, length us, event | category | flops | bytes accessed | tf_op | source)
XLA Modules:
  0.0 145.2 jit_solution(753610515027995251)
XLA Ops:
  1.3 0.0 copy-start
  1.3 142.2 %picard.1 = f32[160,384]{1,0:T(8,128)} custom-call(s32[1]{0:T(128)S(6)} %copy.8.time_any, f32[1]{0:T(128)S(6)} %copy.9.step_any, f32[160,384]{1,0:T(8,128)} %bitcast.5, f32[160,384]{1,0:T(8,128)} %a_any.1, bf16[3,384,384]{2,1,0:T(8,128)(2,1)} %bitcast.4, bf16[384,1536]{1,0:T(8,128)(2,1)} %wi_ref.1, bf16[1536,384]{1,0:T(8,128)(2,1)} %wo_ref.1), custom_call_target="tpu_custom_call" | custom-call | tf_op jit(solution)/shard_map/picard/pallas_call | solution.py:635
  143.5 0.0 copy-done
  143.5 1.7 %add_bitcast_fusion = f32[1,160,384]{2,1,0:T(8,128)} fusion(f32[160,384]{1,0:T(8,128)S(1)} %copy-done, f32[160,384]{1,0:T(8,128)} %picard.1), kind=kLoop, calls=%fused_computation | loop fusion | flops 61440 | bytes 737280 | tf_op jit(solution)/shard_map/broadcast_in_dim | solution.py:646
Async XLA Ops:
  1.3 142.2 %copy-start = (f32[160,384]{1,0:T(8,128)S(1)}, f32[160,384]{1,0:T(8,128)}, u32[]{:S(2)}) copy-start(f32[160,384]{1,0:T(8,128)} %a_any.1) | copy-start | bytes 737284

commit v6 on v5

--- a/solution.py
+++ b/solution.py
@@ -518,9 +518,9 @@
     w_in.spread(3)
     for v in (a, b):
         v.gather(4)
+    w_out.forward()
     w_out.spread(2)
     w_out.spread(1)
-    w_out.forward()
     w_out.spread(3)
     a.gathered()
     b.gathered()

time: 145 us -> 144 us (level)
  Pallas kernels: 142 us -> 140 us
    pallas_call x1, Pallas kernels: 142 us -> 140 us  [local(): pl.pallas_call(kernel, out_shape=jax.ShapeDtypeStruct(anchor.shape, F32),...]
where the time goes in v6:
time: 144 us; the launch traced here: 143 us
  Pallas kernels  140 us (97%)
  other arithmetic  1.66 us (1%)
    pallas_call x1, Pallas kernels, local(): pl.pallas_call(kernel, out_shape=jax.ShapeDtypeStruct(anchor.shape, F32),...  140 us

profile of v6, /device:TPU:17, one launch (start us, length us, event | category | flops | bytes accessed | tf_op | source)
XLA Modules:
  0.0 143.4 jit_solution(13340013319669958984)
XLA Ops:
  1.3 0.0 copy-start
  1.3 140.4 %picard.1 = f32[160,384]{1,0:T(8,128)} custom-call(s32[1]{0:T(128)S(6)} %copy.8.time_any, f32[1]{0:T(128)S(6)} %copy.9.step_any, f32[160,384]{1,0:T(8,128)} %bitcast.5, f32[160,384]{1,0:T(8,128)} %a_any.1, bf16[3,384,384]{2,1,0:T(8,128)(2,1)} %bitcast.4, bf16[384,1536]{1,0:T(8,128)(2,1)} %wi_ref.1, bf16[1536,384]{1,0:T(8,128)(2,1)} %wo_ref.1), custom_call_target="tpu_custom_call" | custom-call | tf_op jit(solution)/shard_map/picard/pallas_call | solution.py:635
  141.7 0.0 copy-done
  141.7 1.7 %add_bitcast_fusion = f32[1,160,384]{2,1,0:T(8,128)} fusion(f32[160,384]{1,0:T(8,128)S(1)} %copy-done, f32[160,384]{1,0:T(8,128)} %picard.1), kind=kLoop, calls=%fused_computation | loop fusion | flops 61440 | bytes 737280 | tf_op jit(solution)/shard_map/broadcast_in_dim | solution.py:646
Async XLA Ops:
  1.3 140.4 %copy-start = (f32[160,384]{1,0:T(8,128)S(1)}, f32[160,384]{1,0:T(8,128)}, u32[]{:S(2)}) copy-start(f32[160,384]{1,0:T(8,128)} %a_any.1) | copy-start | bytes 737284

commit v7 on v6

--- a/solution.py
+++ b/solution.py
@@ -29,7 +29,7 @@
     time_any, step_any, s_ref, a_any, m_any, wi_ref, wo_ref, out_ref,
     time_ref, step_ref, a_ref, m_ref,
     sbuf, abuf, modx, msib, m1, mrecv, modall, win, wout, pref, frecv,
-    stat, statr, xall, hid, obs, obr, part, rss, rsr, dsend, drecv, fsend, drift,
+    stat, statr, xall, hid, obs, obr, part, rss, rsr, dsend, drecv, fsend, drift, acc,
     send, recv,
 ):
     y = lax.axis_index("tm")
@@ -308,11 +308,13 @@
                     put(self.k_ring[s + 1, g, j], slot, slot, dev(z_=zo(sign[g])))
                 put(self.k_sib[s, g, j], slot, slot, sib)
 
-        def gathered(self):
-            for j in range(2):
-                got(self.k_own[j], self.slot(z, 1 - c, j))
+        def gathered(self, steps=(1, 2, 3, 4)):
+            if 1 in steps:
+                for j in range(2):
+                    got(self.k_own[j], self.slot(z, 1 - c, j))
             for (s, g, j), k in self.k_sib.items():
-                got(k, self.slot(zo(-sign[g] * s), 1 - c, j))
+                if s in steps:
+                    got(k, self.slot(zo(-sign[g] * s), 1 - c, j))
 
         def first_matmul(self):
             def tile(n, _):
@@ -327,6 +329,17 @@
             if u[1] < W:
                 return [(j, u[0], u[1]) for j in range(2)]
             return [(None, 256 * n, 256) for n in range(3)]
+
+        def first_half(self, hh, last):
+            rows = pl.ds(pl.multiple_of(hh * (D // 2), 128), D // 2)
+            for n in range(U // 256):
+                cols = slice(256 * n, 256 * n + 256)
+                pre = jnp.dot(self.x[:, rows], win[rows, cols], preferred_element_type=F32)
+                if last:
+                    pre = pre + acc[self.p][:, cols]
+                    self.hid[:, cols] = jax.nn.gelu(pre, approximate=True).astype(BF16)
+                else:
+                    acc[self.p][:, cols] = pre
 
         def second(self, cc, hh, u):
             for j, col, cols in self.tiles(u):
@@ -534,17 +547,16 @@
     for it in range(ITERS):
         a, b = parts[it]
         if it:
-            a.gathered()
-            a.first_matmul()
+            a.gathered((4,))
+            a.first_half(1 - h, True)
         a.second_other(u)
         a.second_own(u)
         if it:
-            b.gather(4)
-            b.gathered()
+            b.gathered((4,))
         a.halves(u)
         a.scatter(1, u)
         if it:
-            b.first_matmul()
+            b.first_half(1 - h, True)
         b.second_other(u)
         b.second_own(u)
         a.scatter(2, u)
@@ -578,7 +590,12 @@
         for s in range(1, 4):
             after.gather(s)
             later.gather(s)
+        after.gathered((1, 2, 3))
+        after.first_half(h, False)
         after.gather(4)
+        later.gathered((1, 2, 3))
+        later.first_half(h, False)
+        later.gather(4)
 
     for copy in pending:
         copy.wait_send()
@@ -629,6 +646,7 @@
         each(lambda n: pltpu.VMEM((3, 2, n, W), BF16)),
         each(lambda n: pltpu.VMEM((2, n, W), BF16)),
         each(lambda n: pltpu.VMEM((2, n, W), F32)),
+        each(lambda n: pltpu.VMEM((4 * n, U), F32)),
         pltpu.SemaphoreType.DMA((COPIES,)),
         pltpu.SemaphoreType.DMA((COPIES,)),
     ]

time: 144 us -> 143 us (level)
  no operation moved by 1% of the time
where the time goes in v7:
time: 143 us
  Pallas kernels  140 us (98%)
  other arithmetic  1.66 us (1%)
    pallas_call x1, Pallas kernels, local(): pl.pallas_call(kernel, out_shape=jax.ShapeDtypeStruct(anchor.shape, F32),...  140 us

profile of v7, /device:TPU:17, one launch (start us, length us, event | category | flops | bytes accessed | tf_op | source)
XLA Modules:
  0.0 142.8 jit_solution(8252895084920707568)
XLA Ops:
  1.3 0.0 copy-start
  1.3 139.8 %picard.1 = f32[160,384]{1,0:T(8,128)} custom-call(s32[1]{0:T(128)S(6)} %copy.8.time_any, f32[1]{0:T(128)S(6)} %copy.9.step_any, f32[160,384]{1,0:T(8,128)} %bitcast.5, f32[160,384]{1,0:T(8,128)} %a_any.1, bf16[3,384,384]{2,1,0:T(8,128)(2,1)} %bitcast.4, bf16[384,1536]{1,0:T(8,128)(2,1)} %wi_ref.1, bf16[1536,384]{1,0:T(8,128)(2,1)} %wo_ref.1), custom_call_target="tpu_custom_call" | custom-call | tf_op jit(solution)/shard_map/picard/pallas_call | solution.py:653
  141.2 0.0 copy-done
  141.2 1.7 %add_bitcast_fusion = f32[1,160,384]{2,1,0:T(8,128)} fusion(f32[160,384]{1,0:T(8,128)S(1)} %copy-done, f32[160,384]{1,0:T(8,128)} %picard.1), kind=kLoop, calls=%fused_computation | loop fusion | flops 61440 | bytes 737280 | tf_op jit(solution)/shard_map/broadcast_in_dim | solution.py:664
Async XLA Ops:
  1.3 139.9 %copy-start = (f32[160,384]{1,0:T(8,128)S(1)}, f32[160,384]{1,0:T(8,128)}, u32[]{:S(2)}) copy-start(f32[160,384]{1,0:T(8,128)} %a_any.1) | copy-start | bytes 737284

commit v8 on v7

--- a/solution.py
+++ b/solution.py
@@ -590,9 +590,9 @@
         for s in range(1, 4):
             after.gather(s)
             later.gather(s)
+        after.gather(4)
         after.gathered((1, 2, 3))
         after.first_half(h, False)
-        after.gather(4)
         later.gathered((1, 2, 3))
         later.first_half(h, False)
         later.gather(4)

time: 143 us -> 143 us (level)
  no operation moved by 1% of the time
where the time goes in v8:
time: 143 us
  Pallas kernels  140 us (98%)
  other arithmetic  1.66 us (1%)
    pallas_call x1, Pallas kernels, local(): pl.pallas_call(kernel, out_shape=jax.ShapeDtypeStruct(anchor.shape, F32),...  140 us

profile of v8, /device:TPU:17, one launch (start us, length us, event | category | flops | bytes accessed | tf_op | source)
XLA Modules:
  0.0 142.8 jit_solution(14352704491329462634)
XLA Ops:
  1.3 0.0 copy-start
  1.3 139.8 %picard.1 = f32[160,384]{1,0:T(8,128)} custom-call(s32[1]{0:T(128)S(6)} %copy.8.time_any, f32[1]{0:T(128)S(6)} %copy.9.step_any, f32[160,384]{1,0:T(8,128)} %bitcast.5, f32[160,384]{1,0:T(8,128)} %a_any.1, bf16[3,384,384]{2,1,0:T(8,128)(2,1)} %bitcast.4, bf16[384,1536]{1,0:T(8,128)(2,1)} %wi_ref.1, bf16[1536,384]{1,0:T(8,128)(2,1)} %wo_ref.1), custom_call_target="tpu_custom_call" | custom-call | tf_op jit(solution)/shard_map/picard/pallas_call | solution.py:653
  141.2 0.0 copy-done
  141.2 1.7 %add_bitcast_fusion = f32[1,160,384]{2,1,0:T(8,128)} fusion(f32[160,384]{1,0:T(8,128)S(1)} %copy-done, f32[160,384]{1,0:T(8,128)} %picard.1), kind=kLoop, calls=%fused_computation | loop fusion | flops 61440 | bytes 737280 | tf_op jit(solution)/shard_map/broadcast_in_dim | solution.py:664
Async XLA Ops:
  1.3 139.9 %copy-start = (f32[160,384]{1,0:T(8,128)S(1)}, f32[160,384]{1,0:T(8,128)}, u32[]{:S(2)}) copy-start(f32[160,384]{1,0:T(8,128)} %a_any.1) | copy-start | bytes 737284
